TPU v7x, 32 devices: a whole 2x2x4 slice. The times are simulated.
32 devices in a mesh: rep: 4 (over y, core), fsdp: 8 (over z, x).
Axes of the slice: x: 2, y: 2, z: 4, core: 2. Of those that a mesh axis runs over, the one named last changes fastest.
Arguments:
- hidden_in: bfloat16 [32, 512, 768], P(('rep', 'fsdp')), may hold values from -6 to 6
- memory: bfloat16 [32, 512, 768], P(('rep', 'fsdp')), may hold values from -6 to 6
- lengths: int32 [32], P(('rep', 'fsdp')), may hold values from 256 to 512, as said below
- buckets: int32 [512], replicated, may hold values from 0 to 31, as said below
- cotangent: bfloat16 [32, 512, 768], P(('rep', 'fsdp')), may hold values from -6 to 6
- self_gain: bfloat16 [768], P('fsdp'), may hold values from 0.099609375 to 1.8984375
- self_query: bfloat16 [768, 768], P('fsdp'), may hold values from -0.02734375 to 0.02734375
- self_key: bfloat16 [768, 768], P('fsdp'), may hold values from -0.21875 to 0.21875
- self_value: bfloat16 [768, 768], P('fsdp'), may hold values from -0.21875 to 0.21875
- self_out: bfloat16 [768, 768], P('fsdp'), may hold values from -0.875 to 0.875
- bias_table: bfloat16 [384], P('fsdp'), may hold values from -4 to 4
- cross_gain: bfloat16 [768], P('fsdp'), may hold values from 0.099609375 to 1.8984375
- cross_query: bfloat16 [768, 768], P('fsdp'), may hold values from -0.02734375 to 0.02734375
- cross_key: bfloat16 [768, 768], P('fsdp'), may hold values from -0.21875 to 0.21875
- cross_value: bfloat16 [768, 768], P('fsdp'), may hold values from -0.21875 to 0.21875
- cross_out: bfloat16 [768, 768], P('fsdp'), may hold values from -0.875 to 0.875
- feed_gain: bfloat16 [768], P('fsdp'), may hold values from 0.099609375 to 1.8984375
- feed_gate: bfloat16 [768, 2048], P('fsdp'), may hold values from -0.21875 to 0.21875
- feed_up: bfloat16 [768, 2048], P('fsdp'), may hold values from -0.21875 to 0.21875
- feed_down: bfloat16 [2048, 768], P('fsdp'), may hold values from -0.125 to 0.125
Outputs:
- layer_out: bfloat16 [32, 512, 768], P(('rep', 'fsdp'))
- input_grad: float32 [32, 512, 768], P(('rep', 'fsdp'))
- memory_grad: float32 [32, 512, 768], P(('rep', 'fsdp'))
- self_gain_grad: float32 [768], P('fsdp')
- self_query_grad: float32 [768, 768], P('fsdp')
- self_key_grad: float32 [768, 768], P('fsdp')
- self_value_grad: float32 [768, 768], P('fsdp')
- self_out_grad: float32 [768, 768], P('fsdp')
- bias_table_grad: float32 [384], P('fsdp')
- cross_gain_grad: float32 [768], P('fsdp')
- cross_query_grad: float32 [768, 768], P('fsdp')
- cross_key_grad: float32 [768, 768], P('fsdp')
- cross_value_grad: float32 [768, 768], P('fsdp')
- cross_out_grad: float32 [768, 768], P('fsdp')
- feed_gain_grad: float32 [768], P('fsdp')
- feed_gate_grad: float32 [768, 2048], P('fsdp')
- feed_up_grad: float32 [768, 2048], P('fsdp')
- feed_down_grad: float32 [2048, 768], P('fsdp')
Inputs may be any that keep to these rules, and one draw needn't show every extreme that they name: `lengths`: every row's length is 256 or 512, and both occur. buckets never fall with the offset, start at 0 at offset 0 and reach 31; every bucket is used.
All inputs are finite; a program needn't handle non-finite values.
Results may differ from a plain program's by a relative error of at most 0.023.
Values may be sent and summed in bfloat16 or wider, within the bound.
No kernel may reach another device: no remote copies, remote signals or barrier semaphores. Data moves between devices by JAX's collectives and lax.ppermute only.
A program may use at most 192 MiB of HBM per device.

v0:
```python
import jax
import jax.numpy as jnp
from jax import lax
from jax.sharding import PartitionSpec as P

HEADS = 12
HEAD = 64
BUCKETS = 32


EPSILON = 1e-06
MASKED = -1e30
PRECISE = lax.Precision.HIGHEST


def project(rows, weight):
    return jnp.einsum("rtd,de->rte", rows, weight, preferred_element_type=jnp.float32)


def project_back(grad, weight):
    return jnp.einsum("rte,de->rtd", grad, weight, preferred_element_type=jnp.float32)


def weight_grad(rows, grad):
    return jnp.einsum("rtd,rte->de", rows, grad, preferred_element_type=jnp.float32)


def norm_forward(hidden, gain):
    scale = lax.rsqrt(jnp.mean(hidden * hidden, axis=-1, keepdims=True) + EPSILON)
    return (hidden * scale * gain, scale)


def norm_backward(hidden, scale, gain, upstream):
    gain_grad = jnp.sum(upstream * (hidden * scale), axis=(0, 1))
    weighted = upstream * gain
    inner = jnp.mean(weighted * hidden, axis=-1, keepdims=True)
    return (scale * weighted - hidden * (scale * scale * scale) * inner, gain_grad)


def smooth_gate(value):
    return jax.nn.gelu(value, approximate=True)


def toeplitz(per_offset):
    heads = per_offset.shape[0]
    length = per_offset.shape[1]
    padded = jnp.concatenate([jnp.zeros((heads, length - 1), jnp.float32), per_offset], axis=1)
    spread = jnp.broadcast_to(padded[:, None, :], (heads, length, 2 * length - 1)).reshape(
        heads, length * (2 * length - 1)
    )
    spread = jnp.concatenate([spread, jnp.zeros((heads, length), jnp.float32)], axis=1).reshape(
        heads, length, 2 * length
    )
    return spread[:, :, length - 1 :: -1]


def diagonal_sums(grid):
    heads = grid.shape[0]
    length = grid.shape[1]
    flipped = grid[:, :, ::-1]
    padded = jnp.concatenate([flipped, jnp.zeros_like(flipped)], axis=2).reshape(
        heads, 2 * length * length
    )
    sheared = padded[:, : length * (2 * length - 1)].reshape(heads, length, 2 * length - 1)
    return jnp.sum(sheared, axis=1)[:, length - 1 :]


def split_pairs(array):
    return array.reshape(array.shape[0], array.shape[1], HEADS // 2, 2, HEAD).transpose(
        2, 0, 1, 3, 4
    )


def join_pairs(array):
    return array.transpose(1, 2, 0, 3, 4).reshape(array.shape[1], array.shape[2], HEADS * HEAD)


def score_block(query, keys, offsets, mask, with_bias):
    scores = jnp.einsum("rihe,rjhe->rhij", query, keys, preferred_element_type=jnp.float32)
    if with_bias:
        scores = scores + toeplitz(offsets)[None]
    return jnp.where(mask, scores, MASKED)


def attend_forward(query, keys, values, offsets, mask, with_bias):

    def one_pair(items):
        pair_query, pair_keys, pair_values, pair_offsets = items
        scores = score_block(pair_query, pair_keys, pair_offsets, mask, with_bias)
        highest = jnp.max(scores, axis=-1, keepdims=True)
        weights = jnp.exp(scores - highest)
        total = jnp.sum(weights, axis=-1, keepdims=True)
        probs = (weights / total).astype(jnp.bfloat16)
        mixed = jnp.einsum(
            "rhij,rjhe->rihe", probs, pair_values, preferred_element_type=jnp.float32
        )
        return (mixed.astype(jnp.bfloat16), (highest + jnp.log(total))[..., 0])

    mixed, logsum = lax.map(
        one_pair,
        (
            split_pairs(query),
            split_pairs(keys),
            split_pairs(values),
            offsets.reshape(HEADS // 2, 2, -1),
        ),
    )
    return (join_pairs(mixed), logsum)


def attend_backward(query, keys, values, offsets, mask, with_bias, logsum, mixed_grad):

    def one_pair(items):
        pair_query, pair_keys, pair_values, pair_offsets, pair_logsum, pair_grad = items
        scores = score_block(pair_query, pair_keys, pair_offsets, mask, with_bias)
        probs = jnp.exp(scores - pair_logsum[..., None])
        prob_grad = jnp.einsum(
            "rihe,rjhe->rhij", pair_grad, pair_values, preferred_element_type=jnp.float32
        )
        delta = jnp.sum(probs * prob_grad, axis=-1, keepdims=True)
        score_grad = (probs * (prob_grad - delta)).astype(jnp.bfloat16)
        query_grad = jnp.einsum(
            "rhij,rjhe->rihe", score_grad, pair_keys, preferred_element_type=jnp.float32
        ).astype(jnp.bfloat16)
        key_grad = jnp.einsum(
            "rhij,rihe->rjhe", score_grad, pair_query, preferred_element_type=jnp.float32
        ).astype(jnp.bfloat16)
        value_grad = jnp.einsum(
            "rhij,rihe->rjhe",
            probs.astype(jnp.bfloat16),
            pair_grad,
            preferred_element_type=jnp.float32,
        ).astype(jnp.bfloat16)
        if with_bias:
            offset_grad = diagonal_sums(jnp.sum(score_grad, axis=0, dtype=jnp.float32))
        else:
            offset_grad = jnp.zeros_like(pair_offsets)
        return (query_grad, key_grad, value_grad, offset_grad)

    query_grad, key_grad, value_grad, offset_grad = lax.map(
        one_pair,
        (
            split_pairs(query),
            split_pairs(keys),
            split_pairs(values),
            offsets.reshape(HEADS // 2, 2, -1),
            logsum,
            split_pairs(mixed_grad),
        ),
    )
    return (
        join_pairs(query_grad),
        join_pairs(key_grad),
        join_pairs(value_grad),
        offset_grad.reshape(HEADS, -1),
    )


def on_device(
    hidden_in,
    memory,
    lengths,
    buckets,
    cotangent,
    self_gain,
    self_query,
    self_key,
    self_value,
    self_out,
    bias_table,
    cross_gain,
    cross_query,
    cross_key,
    cross_value,
    cross_out,
    feed_gain,
    feed_gate,
    feed_up,
    feed_down,
):
    length = hidden_in.shape[1]
    position = jnp.arange(length)
    valid = position[None, :] < lengths[:, None]
    causal = position[None, :] <= position[:, None]
    self_mask = causal[None, None, :, :] & valid[:, None, None, :]
    cross_mask = valid[:, None, None, :]
    picks = (buckets[:, None] == jnp.arange(BUCKETS)[None, :]).astype(jnp.float32)
    no_offsets = jnp.zeros((HEADS, length), jnp.float32)

    def gather_self():
        return (
            lax.all_gather(self_gain, "fsdp", axis=0, tiled=True),
            lax.all_gather(self_query, "fsdp", axis=0, tiled=True),
            lax.all_gather(self_key, "fsdp", axis=0, tiled=True),
            lax.all_gather(self_value, "fsdp", axis=0, tiled=True),
            lax.all_gather(self_out, "fsdp", axis=0, tiled=True),
            lax.all_gather(bias_table, "fsdp", axis=0, tiled=True),
        )

    def gather_cross():
        return (
            lax.all_gather(cross_gain, "fsdp", axis=0, tiled=True),
            lax.all_gather(cross_query, "fsdp", axis=0, tiled=True),
            lax.all_gather(cross_key, "fsdp", axis=0, tiled=True),
            lax.all_gather(cross_value, "fsdp", axis=0, tiled=True),
            lax.all_gather(cross_out, "fsdp", axis=0, tiled=True),
        )

    def gather_feed():
        return (
            lax.all_gather(feed_gain, "fsdp", axis=0, tiled=True),
            lax.all_gather(feed_gate, "fsdp", axis=0, tiled=True),
            lax.all_gather(feed_up, "fsdp", axis=0, tiled=True),
            lax.all_gather(feed_down, "fsdp", axis=0, tiled=True),
        )

    hidden = hidden_in.astype(jnp.float32)
    self_full = gather_self()
    offsets = jnp.dot(
        picks, self_full[5].astype(jnp.float32).reshape(BUCKETS, HEADS), precision=PRECISE
    ).T
    normed_one, scale_one = norm_forward(hidden, self_full[0].astype(jnp.float32))
    normed_one = normed_one.astype(jnp.bfloat16)
    query = project(normed_one, self_full[1]).astype(jnp.bfloat16)
    keys = project(normed_one, self_full[2]).astype(jnp.bfloat16)
    values = project(normed_one, self_full[3]).astype(jnp.bfloat16)
    mixed_one, logsum_one = attend_forward(query, keys, values, offsets, self_mask, True)
    after_self = hidden + project(mixed_one, self_full[4])
    cross_full = gather_cross()
    normed_two, scale_two = norm_forward(after_self, cross_full[0].astype(jnp.float32))
    normed_two = normed_two.astype(jnp.bfloat16)
    cross_queries = project(normed_two, cross_full[1]).astype(jnp.bfloat16)
    memory_keys = project(memory, cross_full[2]).astype(jnp.bfloat16)
    memory_values = project(memory, cross_full[3]).astype(jnp.bfloat16)
    mixed_two, logsum_two = attend_forward(
        cross_queries, memory_keys, memory_values, no_offsets, cross_mask, False
    )
    after_cross = after_self + project(mixed_two, cross_full[4])
    feed_full = gather_feed()
    normed_three, scale_three = norm_forward(after_cross, feed_full[0].astype(jnp.float32))
    normed_three = normed_three.astype(jnp.bfloat16)
    gate = project(normed_three, feed_full[1])
    lift = project(normed_three, feed_full[2])
    activated, gate_back = jax.vjp(smooth_gate, gate)
    inner = (activated * lift).astype(jnp.bfloat16)
    layer_out = (after_cross + project(inner, feed_full[3])).astype(jnp.bfloat16)
    upstream = cotangent.astype(jnp.float32)
    feed_back = gather_feed()
    inner_grad = project_back(cotangent, feed_back[3])
    down_grad = weight_grad(inner, cotangent)
    gate_grad = gate_back(inner_grad * lift)[0].astype(jnp.bfloat16)
    lift_grad = (inner_grad * activated).astype(jnp.bfloat16)
    gate_weight_grad = weight_grad(normed_three, gate_grad)
    lift_weight_grad = weight_grad(normed_three, lift_grad)
    normed_grad = project_back(gate_grad, feed_back[1]) + project_back(lift_grad, feed_back[2])
    residual_grad, gain_three_grad = norm_backward(
        after_cross, scale_three, feed_back[0].astype(jnp.float32), normed_grad
    )
    carried = upstream + residual_grad
    feed_grads = (gain_three_grad, gate_weight_grad, lift_weight_grad, down_grad)
    feed_grads = (
        lax.psum_scatter(gain_three_grad, "fsdp", scatter_dimension=0, tiled=True),
        lax.psum_scatter(gate_weight_grad, "fsdp", scatter_dimension=0, tiled=True),
        lax.psum_scatter(lift_weight_grad, "fsdp", scatter_dimension=0, tiled=True),
        lax.psum_scatter(down_grad, "fsdp", scatter_dimension=0, tiled=True),
    )
    cross_back = gather_cross()
    branch_two = carried.astype(jnp.bfloat16)
    cross_out_weight_grad = weight_grad(mixed_two, branch_two)
    mixed_two_grad = project_back(branch_two, cross_back[4]).astype(jnp.bfloat16)
    cross_queries_grad, memory_keys_grad, memory_values_grad, spare = attend_backward(
        cross_queries,
        memory_keys,
        memory_values,
        no_offsets,
        cross_mask,
        False,
        logsum_two,
        mixed_two_grad,
    )
    memory_grad = project_back(memory_keys_grad, cross_back[2]) + project_back(
        memory_values_grad, cross_back[3]
    )
    normed_grad = project_back(cross_queries_grad, cross_back[1])
    residual_grad, gain_two_grad = norm_backward(
        after_self, scale_two, cross_back[0].astype(jnp.float32), normed_grad
    )
    carried = carried + residual_grad
    cross_query_weight_grad = weight_grad(normed_two, cross_queries_grad)
    cross_key_weight_grad = weight_grad(memory, memory_keys_grad)
    cross_value_weight_grad = weight_grad(memory, memory_values_grad)
    cross_grads = (
        gain_two_grad,
        cross_query_weight_grad,
        cross_key_weight_grad,
        cross_value_weight_grad,
        cross_out_weight_grad,
    )
    cross_grads = (
        lax.psum_scatter(gain_two_grad, "fsdp", scatter_dimension=0, tiled=True),
        lax.psum_scatter(cross_query_weight_grad, "fsdp", scatter_dimension=0, tiled=True),
        lax.psum_scatter(cross_key_weight_grad, "fsdp", scatter_dimension=0, tiled=True),
        lax.psum_scatter(cross_value_weight_grad, "fsdp", scatter_dimension=0, tiled=True),
        lax.psum_scatter(cross_out_weight_grad, "fsdp", scatter_dimension=0, tiled=True),
    )
    self_back = gather_self()
    branch_one = carried.astype(jnp.bfloat16)
    self_out_weight_grad = weight_grad(mixed_one, branch_one)
    mixed_one_grad = project_back(branch_one, self_back[4]).astype(jnp.bfloat16)
    query_grad, keys_grad, values_grad, offset_grad = attend_backward(
        query, keys, values, offsets, self_mask, True, logsum_one, mixed_one_grad
    )
    normed_grad = (
        project_back(query_grad, self_back[1])
        + project_back(keys_grad, self_back[2])
        + project_back(values_grad, self_back[3])
    )
    residual_grad, gain_one_grad = norm_backward(
        hidden, scale_one, self_back[0].astype(jnp.float32), normed_grad
    )
    input_grad = carried + residual_grad
    table_grad = jnp.dot(picks.T, offset_grad.T, precision=PRECISE).reshape(-1)
    self_query_weight_grad = weight_grad(normed_one, query_grad)
    self_key_weight_grad = weight_grad(normed_one, keys_grad)
    self_value_weight_grad = weight_grad(normed_one, values_grad)
    self_grads = (
        gain_one_grad,
        self_query_weight_grad,
        self_key_weight_grad,
        self_value_weight_grad,
        self_out_weight_grad,
        table_grad,
    )
    self_grads = (
        lax.psum_scatter(gain_one_grad, "fsdp", scatter_dimension=0, tiled=True),
        lax.psum_scatter(self_query_weight_grad, "fsdp", scatter_dimension=0, tiled=True),
        lax.psum_scatter(self_key_weight_grad, "fsdp", scatter_dimension=0, tiled=True),
        lax.psum_scatter(self_value_weight_grad, "fsdp", scatter_dimension=0, tiled=True),
        lax.psum_scatter(self_out_weight_grad, "fsdp", scatter_dimension=0, tiled=True),
        lax.psum_scatter(table_grad, "fsdp", scatter_dimension=0, tiled=True),
    )
    shards = tuple(self_grads) + tuple(cross_grads) + tuple(feed_grads)
    columns = (
        lax.psum_scatter(
            shards[1].astype(jnp.bfloat16), "rep", scatter_dimension=1, tiled=True
        ).astype(jnp.float32),
        lax.psum_scatter(
            shards[2].astype(jnp.bfloat16), "rep", scatter_dimension=1, tiled=True
        ).astype(jnp.float32),
        lax.psum_scatter(
            shards[3].astype(jnp.bfloat16), "rep", scatter_dimension=1, tiled=True
        ).astype(jnp.float32),
        lax.psum_scatter(
            shards[4].astype(jnp.bfloat16), "rep", scatter_dimension=1, tiled=True
        ).astype(jnp.float32),
        lax.psum_scatter(
            shards[7].astype(jnp.bfloat16), "rep", scatter_dimension=1, tiled=True
        ).astype(jnp.float32),
        lax.psum_scatter(
            shards[8].astype(jnp.bfloat16), "rep", scatter_dimension=1, tiled=True
        ).astype(jnp.float32),
        lax.psum_scatter(
            shards[9].astype(jnp.bfloat16), "rep", scatter_dimension=1, tiled=True
        ).astype(jnp.float32),
        lax.psum_scatter(
            shards[10].astype(jnp.bfloat16), "rep", scatter_dimension=1, tiled=True
        ).astype(jnp.float32),
        lax.psum_scatter(
            shards[12].astype(jnp.bfloat16), "rep", scatter_dimension=1, tiled=True
        ).astype(jnp.float32),
        lax.psum_scatter(
            shards[13].astype(jnp.bfloat16), "rep", scatter_dimension=1, tiled=True
        ).astype(jnp.float32),
        lax.psum_scatter(
            shards[14].astype(jnp.bfloat16), "rep", scatter_dimension=1, tiled=True
        ).astype(jnp.float32),
    )
    matrices = (
        lax.all_gather(columns[0].astype(jnp.bfloat16), "rep", axis=1, tiled=True).astype(
            jnp.float32
        ),
        lax.all_gather(columns[1].astype(jnp.bfloat16), "rep", axis=1, tiled=True).astype(
            jnp.float32
        ),
        lax.all_gather(columns[2].astype(jnp.bfloat16), "rep", axis=1, tiled=True).astype(
            jnp.float32
        ),
        lax.all_gather(columns[3].astype(jnp.bfloat16), "rep", axis=1, tiled=True).astype(
            jnp.float32
        ),
        lax.all_gather(columns[4].astype(jnp.bfloat16), "rep", axis=1, tiled=True).astype(
            jnp.float32
        ),
        lax.all_gather(columns[5].astype(jnp.bfloat16), "rep", axis=1, tiled=True).astype(
            jnp.float32
        ),
        lax.all_gather(columns[6].astype(jnp.bfloat16), "rep", axis=1, tiled=True).astype(
            jnp.float32
        ),
        lax.all_gather(columns[7].astype(jnp.bfloat16), "rep", axis=1, tiled=True).astype(
            jnp.float32
        ),
        lax.all_gather(columns[8].astype(jnp.bfloat16), "rep", axis=1, tiled=True).astype(
            jnp.float32
        ),
        lax.all_gather(columns[9].astype(jnp.bfloat16), "rep", axis=1, tiled=True).astype(
            jnp.float32
        ),
        lax.all_gather(columns[10].astype(jnp.bfloat16), "rep", axis=1, tiled=True).astype(
            jnp.float32
        ),
    )
    smalls = lax.psum((shards[0], shards[5], shards[6], shards[11]), "rep")
    return (
        layer_out,
        input_grad,
        memory_grad,
        smalls[0],
        matrices[0],
        matrices[1],
        matrices[2],
        matrices[3],
        smalls[1],
        smalls[2],
        matrices[4],
        matrices[5],
        matrices[6],
        matrices[7],
        smalls[3],
        matrices[8],
        matrices[9],
        matrices[10],
    )


def solution(mesh):
    placed = (
        P(("rep", "fsdp"), None, None),
        P(("rep", "fsdp"), None, None),
        P(("rep", "fsdp")),
        P(),
        P(("rep", "fsdp"), None, None),
        P("fsdp"),
        P("fsdp", None),
        P("fsdp", None),
        P("fsdp", None),
        P("fsdp", None),
        P("fsdp"),
        P("fsdp"),
        P("fsdp", None),
        P("fsdp", None),
        P("fsdp", None),
        P("fsdp", None),
        P("fsdp"),
        P("fsdp", None),
        P("fsdp", None),
        P("fsdp", None),
    )
    return jax.shard_map(
        on_device,
        mesh=mesh,
        in_specs=placed,
        out_specs=(
            P(("rep", "fsdp"), None, None),
            P(("rep", "fsdp"), None, None),
            P(("rep", "fsdp"), None, None),
            P("fsdp"),
            P("fsdp", None),
            P("fsdp", None),
            P("fsdp", None),
            P("fsdp", None),
            P("fsdp"),
            P("fsdp"),
            P("fsdp", None),
            P("fsdp", None),
            P("fsdp", None),
            P("fsdp", None),
            P("fsdp"),
            P("fsdp", None),
            P("fsdp", None),
            P("fsdp", None),
        ),
        check_vma=False,
    )
```

profile of v0, /device:TPU:0, one launch (start us, length us, event | category | flops | bytes accessed | tf_op | source)
XLA Modules:
  0.0 2222.3 jit_solution(16175530425375875888)
XLA Ops:
  17.7 23.5 %all-reduce.15 = (bf16[768]{0:T(1024)(128)(2,1)S(1)}, bf16[384]{0:T(512)(128)(2,1)S(1)}, bf16[768]{0:T(1024)(128)(2,1)S(1)}, bf16[768]{0:T(1024)(128)(2,1)S(1)}) all-reduce(bf16[768]{0:T(1024)(128)(2,1)S(1)} %dynamic-update-slice, bf16[384]{0:T(512)(128)(2,1)S(1)} %dynamic-update-slice.1, ...), channel_id=1, replica_groups=mesh['rep'=4,'fsdp'=8] {'fsdp'}, use_global_device_ids=true, to_apply=%add.5 | all-reduce | flops 2688 | bytes 10752
  57.5 38.8 %all-gather.12.cloned.1.call-done = bf16[768,768]{1,0:T(8,128)(2,1)} async-done(((bf16[96,768]{1,0:T(8,128)(2,1)}), bf16[768,768]{1,0:T(8,128)(2,1)}) %all-gather.12.cloned.1.call-update) | async-done | bytes 1179664 | tf_op jit(solution)/shard_map/all_gather | solution.py:195
  99.6 38.8 %all-gather.14.cloned.1.call-done = bf16[768,768]{1,0:T(8,128)(2,1)} async-done(((bf16[96,768]{1,0:T(8,128)(2,1)}), bf16[768,768]{1,0:T(8,128)(2,1)}) %all-gather.14.cloned.1.call-update) | async-done | bytes 1179664 | tf_op jit(solution)/shard_map/all_gather | solution.py:193
  142.6 224.5 %while.58 = (s32[]{:T(128)}, bf16[6,1,512,2,64]{2,4,3,1,0:T(8,128)(2,1)}, f32[6,1,2,512]{3,2,1,0:T(2,128)S(1)}, bf16[6,1,512,2,64]{2,4,3,1,0:T(8,128)(2,1)}, bf1...) while((s32[]{:T(128)}, ...), condition=%wide.region_4.5_spmd.clone, body=%wide.region_1.4_spmd.clone.sunk | while | flops 139000832 | bytes 51427940 | solution.py:99
  385.7 28.7 %while.59 = (s32[]{:T(128)}, bf16[6,1,512,2,64]{2,4,3,1,0:T(8,128)(2,1)}, f32[6,1,2,512]{3,2,1,0:T(2,128)S(1)}, bf16[6,1,512,2,64]{2,4,3,1,0:T(8,128)(2,1)}, bf1...) while((s32[]{:T(128)}, ...), condition=%wide.region_9.10_spmd.clone, body=%wide.region_6.9_spmd.clone.sunk | while | flops 139001344 | bytes 6852701 | solution.py:99
  425.0 45.8 %all-gather.30.cloned.1.call-done = bf16[768,2048]{1,0:T(8,128)(2,1)} async-done(((bf16[96,2048]{1,0:T(8,128)(2,1)}), bf16[768,2048]{1,0:T(8,128)(2,1)}) %all-gather.30.cloned.1.call-update) | async-done | bytes 3145744 | tf_op jit(solution)/shard_map/all_gather | solution.py:213
  476.7 55.3 %all-gather.32.cloned.1.call-done = bf16[2048,768]{1,0:T(8,128)(2,1)} async-done(((bf16[256,768]{1,0:T(8,128)(2,1)}), bf16[2048,768]{1,0:T(8,128)(2,1)}) %all-gather.32.cloned.1.call-update) | async-done | bytes 3145744 | tf_op jit(solution)/shard_map/all_gather | solution.py:214
  556.9 55.8 %while.60 = (s32[]{:T(128)}, bf16[6,1,512,2,64]{2,4,3,1,0:T(8,128)(2,1)}, bf16[6,1,512,2,64]{2,4,3,1,0:T(8,128)(2,1)}, bf16[6,1,512,2,64]{2,4,3,1,0:T(8,128)(2,1...) while((s32[]{:T(128)}, ...), condition=%wide.region_14.15_spmd.clone, body=%wide.region_12.14_spmd.clone.sunk | while | flops 339934720 | bytes 17066100 | solution.py:140
  631.4 534.6 %while.61 = (s32[]{:T(128)}, bf16[6,1,512,2,64]{2,4,3,1,0:T(8,128)(2,1)}, bf16[6,1,512,2,64]{2,4,3,1,0:T(8,128)(2,1)}, bf16[6,1,512,2,64]{2,4,3,1,0:T(8,128)(2,1...) while((s32[]{:T(128)}, ...), condition=%wide.region_19.20_spmd.clone, body=%wide.region_16.19_spmd.clone.sunk | while | flops 342028288 | bytes 117212856 | solution.py:140
  654.0 16.7 rev.16
  675.8 15.7 rev.17
  743.1 16.7 rev.16
  832.1 16.7 rev.16
  921.0 16.7 rev.16
  1010.0 16.7 rev.16
  1098.9 16.7 rev.16
  1219.1 18.4 reduce-scatter.41.cloned.1.call-done
  1239.4 69.6 %reduce-scatter.43.cloned.1.call-done = f32[96,768]{1,0:T(8,128)} async-done(((f32[768,768]{1,0:T(8,128)}), f32[96,768]{1,0:T(8,128)}) %reduce-scatter.43.cloned.1.call-update) | async-done | bytes 294928 | tf_op jit(solution)/shard_map/reduce_scatter | solution.py:337
  1310.9 69.6 %reduce-scatter.45.cloned.1.call-done = f32[96,768]{1,0:T(8,128)} async-done(((f32[768,768]{1,0:T(8,128)}), f32[96,768]{1,0:T(8,128)}) %reduce-scatter.45.cloned.1.call-update) | async-done | bytes 294928 | tf_op jit(solution)/shard_map/reduce_scatter | solution.py:338
  1383.6 68.3 %reduce-scatter.55.cloned.1.call-done = f32[96,768]{1,0:T(8,128)} async-done(((f32[768,768]{1,0:T(8,128)}), f32[96,768]{1,0:T(8,128)}) %reduce-scatter.55.cloned.1.call-update) | async-done | bytes 294928 | tf_op jit(solution)/shard_map/reduce_scatter | solution.py:304
  1457.2 66.2 %reduce-scatter.77.cloned.1.call-done = f32[96,768]{1,0:T(8,128)} async-done(((f32[768,768]{1,0:T(8,128)}), f32[96,768]{1,0:T(8,128)}) %reduce-scatter.77.cloned.1.call-update) | async-done | bytes 294928
  1528.5 66.6 %reduce-scatter.79.cloned.1.call-done = f32[96,768]{1,0:T(8,128)} async-done(((f32[768,768]{1,0:T(8,128)}), f32[96,768]{1,0:T(8,128)}) %reduce-scatter.79.cloned.1.call-update) | async-done | bytes 294928
  1600.5 115.0 %reduce-scatter.57.cloned.1.call-done = f32[96,2048]{1,0:T(8,128)} async-done(((f32[768,2048]{1,0:T(8,128)}), f32[96,2048]{1,0:T(8,128)}) %reduce-scatter.57.cloned.1.call-update) | async-done | bytes 786448 | tf_op jit(solution)/shard_map/reduce_scatter | solution.py:263
  1723.4 112.9 %reduce-scatter.61.cloned.1.call-done = f32[96,2048]{1,0:T(8,128)} async-done(((f32[768,2048]{1,0:T(8,128)}), f32[96,2048]{1,0:T(8,128)}) %reduce-scatter.61.cloned.1.call-update) | async-done | bytes 786448 | tf_op jit(solution)/shard_map/reduce_scatter | solution.py:264
  1846.7 110.3 %reduce-scatter.65.cloned.1.call-done = f32[256,768]{1,0:T(8,128)} async-done(((f32[2048,768]{1,0:T(8,128)}), f32[256,768]{1,0:T(8,128)}) %reduce-scatter.65.cloned.1.call-update) | async-done | bytes 786448 | tf_op jit(solution)/shard_map/reduce_scatter | solution.py:265
  1959.7 35.3 %all-reduce.13 = (f32[768]{0:T(1024)S(1)}, f32[384]{0:T(512)S(1)}, f32[768]{0:T(1024)S(1)}, f32[768]{0:T(1024)S(1)}) all-reduce(f32[768]{0:T(1024)S(1)} %get-tuple-element.447, f32[384]{0:T(512)S(1)} %reshape.697, f32[768]{0:T(1024)S(1)} %copy-done.35, f32[768]{0:T(1024)S(1)} %copy-done.34), channel_id=2, replica_groups=mesh['rep'=4,'fsdp'=8] {'fsdp'}, use_global_device_ids=true, to_apply=%region_22.23.clone | all-reduce | flops 2688 | bytes 21504
  2031.1 16.0 reduce-scatter.69.cloned.1.call-done
  2053.7 16.0 reduce-scatter.71.cloned.1.call-done
  2098.6 16.1 reduce-scatter.51.cloned.1.call-done
  2143.4 17.3 reduce-scatter.59.cloned.1.call-done
  2168.0 16.7 reduce-scatter.63.cloned.1.call-done
  2192.0 15.9 reduce-scatter.83.cloned.1.call-done
  (626 shorter events, 1053.5 us)
Async XLA Ops:
  8.0 88.3 %all-gather.12.cloned.1.call-start = ((), (), s32[]{:S(2)}) async-start(), calls=%async_computation.22 | async-start | bytes 1327104 | tf_op jit(solution)/shard_map/all_gather | solution.py:195
  8.8 129.6 %all-gather.14.cloned.1.call-start = ((), (), s32[]{:S(2)}) async-start(), calls=%async_computation.23 | async-start | bytes 1327104 | tf_op jit(solution)/shard_map/all_gather | solution.py:193
  9.5 357.6 %all-gather.18.cloned.1.call-start = ((), (), s32[]{:S(2)}) async-start(), calls=%async_computation.25 | async-start | bytes 1327104 | tf_op jit(solution)/shard_map/all_gather | solution.py:196
  10.1 359.7 %all-gather.22.cloned.1.call-start = ((), (), s32[]{:S(2)}) async-start(), calls=%async_computation.27 | async-start | bytes 1327104 | tf_op jit(solution)/shard_map/all_gather | solution.py:203
  10.7 363.6 %all-gather.20.cloned.1.call-start = ((), (), s32[]{:S(2)}) async-start(), calls=%async_computation.26 | async-start | bytes 1327104 | tf_op jit(solution)/shard_map/all_gather | solution.py:205
  11.2 368.3 %all-gather.24.cloned.1.call-start = ((), (), s32[]{:S(2)}) async-start(), calls=%async_computation.28 | async-start | bytes 1327104 | tf_op jit(solution)/shard_map/all_gather | solution.py:204
  12.0 402.4 %all-gather.26.cloned.1.call-start = ((), (), s32[]{:S(2)}) async-start(), calls=%async_computation.29 | async-start | bytes 1327104 | tf_op jit(solution)/shard_map/all_gather | solution.py:206
  12.7 406.3 %all-gather.28.cloned.1.call-start = ((), (), s32[]{:S(2)}) async-start(), calls=%async_computation.30 | async-start | bytes 3538944 | tf_op jit(solution)/shard_map/all_gather | solution.py:212
  13.5 457.3 %all-gather.30.cloned.1.call-start = ((), (), s32[]{:S(2)}) async-start(), calls=%async_computation.31 | async-start | bytes 3538944 | tf_op jit(solution)/shard_map/all_gather | solution.py:213
  14.1 518.0 %all-gather.32.cloned.1.call-start = ((), (), s32[]{:S(2)}) async-start(), calls=%async_computation.32 | async-start | bytes 3538944 | tf_op jit(solution)/shard_map/all_gather | solution.py:214
  14.8 1200.5 %reduce-scatter.49.cloned.1.call-start = ((), (), s32[]{:S(2)}) async-start(), calls=%async_computation.37 | async-start | bytes 2654208 | tf_op jit(solution)/shard_map/reduce_scatter | solution.py:301
  616.2 601.0 %reduce-scatter.47.cloned.1.call-start = ((), (), s32[]{:S(2)}) async-start(), calls=%async_computation.36 | async-start | bytes 2654208 | tf_op jit(solution)/shard_map/reduce_scatter | solution.py:339
  628.4 609.2 %reduce-scatter.41.cloned.1.call-start = ((), (), s32[]{:S(2)}) async-start(), calls=%async_computation.33 | async-start | bytes 2654208 | tf_op jit(solution)/shard_map/reduce_scatter | solution.py:336
  1169.7 139.3 %reduce-scatter.43.cloned.1.call-start = ((), (), s32[]{:S(2)}) async-start(), calls=%async_computation.34 | async-start | bytes 2654208 | tf_op jit(solution)/shard_map/reduce_scatter | solution.py:337
  1173.5 207.0 %reduce-scatter.45.cloned.1.call-start = ((), (), s32[]{:S(2)}) async-start(), calls=%async_computation.35 | async-start | bytes 2654208 | tf_op jit(solution)/shard_map/reduce_scatter | solution.py:338
  1177.1 274.8 %reduce-scatter.55.cloned.1.call-start = ((), (), s32[]{:S(2)}) async-start(), calls=%async_computation.40 | async-start | bytes 2654208 | tf_op jit(solution)/shard_map/reduce_scatter | solution.py:304
  1181.8 341.6 %reduce-scatter.77.cloned.1.call-start = ((), (), s32[]{:S(2)}) async-start(), calls=%async_computation.51 | async-start | bytes 2654208
  1188.2 406.8 %reduce-scatter.79.cloned.1.call-start = ((), (), s32[]{:S(2)}) async-start(), calls=%async_computation.52 | async-start | bytes 2654208
  1194.7 520.9 %reduce-scatter.57.cloned.1.call-start = ((), (), s32[]{:S(2)}) async-start(), calls=%async_computation.41 | async-start | bytes 7077888 | tf_op jit(solution)/shard_map/reduce_scatter | solution.py:263
  1201.9 634.4 %reduce-scatter.61.cloned.1.call-start = ((), (), s32[]{:S(2)}) async-start(), calls=%async_computation.43 | async-start | bytes 7077888 | tf_op jit(solution)/shard_map/reduce_scatter | solution.py:264
  1208.0 749.0 %reduce-scatter.65.cloned.1.call-start = ((), (), s32[]{:S(2)}) async-start(), calls=%async_computation.45 | async-start | bytes 7077888 | tf_op jit(solution)/shard_map/reduce_scatter | solution.py:265
  1215.2 786.2 %reduce-scatter.75.cloned.1.call-start = ((), (), s32[]{:S(2)}) async-start(), calls=%async_computation.50 | async-start | bytes 245760
  1217.1 790.9 %reduce-scatter.73.cloned.1.call-start = ((), (), s32[]{:S(2)}) async-start(), calls=%async_computation.49 | async-start | bytes 245760
  1219.0 805.4 %reduce-scatter.67.cloned.1.call-start = ((), (), s32[]{:S(2)}) async-start(), calls=%async_computation.46 | async-start | bytes 245760
  1239.4 807.7 %reduce-scatter.69.cloned.1.call-start = ((), (), s32[]{:S(2)}) async-start(), calls=%async_computation.47 | async-start | bytes 245760
  1310.9 758.8 %reduce-scatter.71.cloned.1.call-start = ((), (), s32[]{:S(2)}) async-start(), calls=%async_computation.48 | async-start | bytes 245760
  1382.3 709.6 %reduce-scatter.81.cloned.1.call-start = ((), (), s32[]{:S(2)}) async-start(), calls=%async_computation.53 | async-start | bytes 245760
  1453.7 661.0 %reduce-scatter.51.cloned.1.call-start = ((), (), s32[]{:S(2)}) async-start(), calls=%async_computation.38 | async-start | bytes 245760 | tf_op jit(solution)/shard_map/reduce_scatter | solution.py:359
  1525.2 611.6 %reduce-scatter.53.cloned.1.call-start = ((), (), s32[]{:S(2)}) async-start(), calls=%async_computation.39 | async-start | bytes 245760 | tf_op jit(solution)/shard_map/reduce_scatter | solution.py:362
  1596.8 563.9 %reduce-scatter.59.cloned.1.call-start = ((), (), s32[]{:S(2)}) async-start(), calls=%async_computation.42 | async-start | bytes 491520 | tf_op jit(solution)/shard_map/reduce_scatter | solution.py:368
  1717.5 467.2 %reduce-scatter.63.cloned.1.call-start = ((), (), s32[]{:S(2)}) async-start(), calls=%async_computation.44 | async-start | bytes 491520 | tf_op jit(solution)/shard_map/reduce_scatter | solution.py:371
  1838.2 369.6 %reduce-scatter.83.cloned.1.call-start = ((), (), s32[]{:S(2)}) async-start(), calls=%async_computation.54 | async-start | bytes 491520
  (57 other events, 2742.2 us)
Sparse Core Ops, SparseCore 0:
  10.3 43.9 all-gather.15
  56.4 39.8 all-gather.11
  98.5 39.8 all-gather.13
  140.4 39.8 all-gather.17
  182.3 39.8 all-gather.21
  224.2 39.8 all-gather.19
  266.2 39.8 all-gather.23
  308.3 39.8 all-gather.25
  350.4 59.2 all-gather.27
  411.7 59.0 all-gather.29
  473.0 59.0 all-gather.31
  616.3 67.5 reduce-scatter.48
  687.4 68.0 reduce-scatter.46
  1169.9 67.6 reduce-scatter.40
  1240.9 68.1 reduce-scatter.42
  1312.4 68.0 reduce-scatter.44
  1383.8 68.0 reduce-scatter.54
  1455.2 68.0 reduce-scatter.76
  1526.9 68.1 reduce-scatter.78
  1598.4 117.0 reduce-scatter.56
  1719.1 117.0 reduce-scatter.60
  1839.9 117.1 reduce-scatter.64
  1981.8 19.7 reduce-scatter.72
  2004.7 19.7 reduce-scatter.66
  2027.3 19.7 reduce-scatter.68
  2049.9 19.7 reduce-scatter.70
  2072.1 19.7 reduce-scatter.80
  2094.9 19.7 reduce-scatter.50
  2117.0 19.7 reduce-scatter.52
  2139.9 20.8 reduce-scatter.58
  2163.8 20.8 reduce-scatter.62
  2187.0 20.7 reduce-scatter.82
  (1 shorter events, 18.8 us)
where the time goes:
time: 2250 us; the launch traced here: 2220 us
  waiting for transfers between devices  1030 us (46%)
  local copies, waits for them, and re-layouts  693 us (31%)
  matrix products  285 us (13%)
  blocking collectives  130 us (6%)
  other arithmetic  58.8 us (3%)
    unnamed x42, waiting for transfers between devices  213 us
    rev x12, local copies, waits for them, and re-layouts, toeplitz(): return spread[:, :, length - 1::-1]  182 us
    reshape x12, local copies, waits for them, and re-layouts, toeplitz(): jnp.broadcast_to(padded[:, None, :], (heads, length, 2 * length - 1))  118 us
    reduce_scatter x1, waiting for transfers between devices, on_device(): lax.psum_scatter(gate_weight_grad, 'fsdp', scatter_dimension=0, tiled=True)  115 us
    reduce_scatter x1, waiting for transfers between devices, on_device(): lax.psum_scatter(lift_weight_grad, 'fsdp', scatter_dimension=0, tiled=True)  113 us
    reduce_scatter x1, waiting for transfers between devices, on_device(): lax.psum_scatter(down_grad, 'fsdp', scatter_dimension=0, tiled=True)  110 us
    rev x6, local copies, waits for them, and re-layouts, diagonal_sums(): flipped = grid[:, :, ::-1]  94.4 us
    while x66, local copies, waits for them, and re-layouts  87.7 us
  transfers between devices with their start and end apart: 33, of which 23 were waited for; matrix products, arithmetic and copies ran while one was open for 42% of the time, Pallas kernels for 0%

commit v1 on v0

v1 whole, which is shorter than its diff:
```python
import functools
import jax
import jax.numpy as jnp
from jax import lax
from jax.experimental import pallas as pl
from jax.experimental.pallas import tpu as pltpu
from jax.sharding import PartitionSpec as P

HEADS = 12
HEAD = 64
BUCKETS = 32
EPSILON = 1e-06
MASKED = -1e30
PRECISE = lax.Precision.HIGHEST
VMEM = 48 * 1024 * 1024
F32 = jnp.float32
BF16 = jnp.bfloat16
NT = (((1,), (1,)), ((), ()))
NN = (((1,), (0,)), ((), ()))
TN = (((0,), (0,)), ((), ()))
TILE = 128


def dot(a, b, dims):
    return lax.dot_general(a, b, dims, preferred_element_type=F32)


def bias_tiles(offs, length):
    base = pltpu.roll(jnp.broadcast_to(offs, (TILE, length)), 0, 1, stride=1, stride_axis=0)
    return jnp.concatenate([base[:, length - TILE :], base], axis=1)


def diagonal_sums(spread, length):
    total = spread[:8]
    for at in range(8, TILE, 8):
        total = total + pltpu.roll(spread[at : at + 8], length - at, 1)
    row = lax.broadcasted_iota(jnp.int32, total.shape, 0)
    for bit in (1, 2, 4):
        total = jnp.where((row & bit) != 0, pltpu.roll(total, length - bit, 1), total)
    return jnp.sum(total, axis=0, keepdims=True)


def bias_block(tiles, first, rows, step):
    parts = []
    for block in range(rows // TILE):
        at = first - block * TILE + TILE
        parts.append(tiles[:, at : at + step])
    return jnp.concatenate(parts, axis=0)


def allowed(rows, step, first, length, causal):
    key = lax.broadcasted_iota(jnp.int32, (rows, step), 0)
    ok = key < length
    if causal:
        item = lax.broadcasted_iota(jnp.int32, (rows, step), 1) + first
        ok = ok & (key <= item)
    return ok


def forward_kernel(causal, lengths, *refs):
    if causal:
        offs_ref, q_ref, k_ref, v_ref, mixed_ref, lse_ref = refs
    else:
        q_ref, k_ref, v_ref, mixed_ref, lse_ref = refs
    size = q_ref.shape[0]
    step = 256
    length = lengths[0]
    for head in range(2):
        cols = slice(head * HEAD, (head + 1) * HEAD)
        if causal:
            tiles = bias_tiles(offs_ref[0, head : head + 1, :], size)
        for first in range(0, size, step):
            rows = first + step if causal else size
            scores = dot(k_ref[:rows, cols], q_ref[first : first + step, cols], NT)
            if causal:
                scores = scores + bias_block(tiles, first, rows, step)
            scores = jnp.where(allowed(rows, step, first, length, causal), scores, MASKED)
            highest = jnp.max(scores, axis=0, keepdims=True)
            weights = jnp.exp(scores - highest)
            total = jnp.sum(weights, axis=0, keepdims=True)
            mixed = dot(v_ref[:rows, cols], weights.astype(BF16), TN) * (1.0 / total)
            mixed_ref[first : first + step, cols] = mixed.T.astype(BF16)
            lse_ref[0, head : head + 1, first : first + step] = highest + jnp.log(total)


def backward_kernel(causal, lengths, *refs):
    if causal:
        offs_ref, q_ref, k_ref, v_ref, g_ref, lse_ref, dq_ref, dk_ref, dv_ref, doffs_ref = refs
    else:
        q_ref, k_ref, v_ref, g_ref, lse_ref, dq_ref, dk_ref, dv_ref = refs
    size = q_ref.shape[0]
    step = 256
    length = lengths[0]
    for head in range(2):
        cols = slice(head * HEAD, (head + 1) * HEAD)
        if causal:
            tiles = bias_tiles(offs_ref[0, head : head + 1, :], size)
            spread = [jnp.zeros((TILE, TILE), F32) for _ in range(size // TILE)]
        dk = [None] * (size // step)
        dv = [None] * (size // step)
        for first in range(0, size, step):
            rows = first + step if causal else size
            q = q_ref[first : first + step, cols]
            g = g_ref[first : first + step, cols]
            k = k_ref[:rows, cols]
            scores = dot(k, q, NT)
            if causal:
                scores = scores + bias_block(tiles, first, rows, step)
            scores = jnp.where(allowed(rows, step, first, length, causal), scores, MASKED)
            probs = jnp.exp(scores - lse_ref[0, head : head + 1, first : first + step])
            prob_grad = dot(v_ref[:rows, cols], g, NT)
            delta = jnp.sum(probs * prob_grad, axis=0, keepdims=True)
            score_grad = (probs * (prob_grad - delta)).astype(BF16)
            if causal:
                for block in range(rows // TILE):
                    for lane in range(step // TILE):
                        at = first // TILE + lane - block
                        if at >= 0:
                            spread[at] = spread[at] + score_grad[
                                block * TILE : (block + 1) * TILE, lane * TILE : (lane + 1) * TILE
                            ].astype(F32)
            dk_now = dot(score_grad, q, NN)
            dv_now = dot(probs.astype(BF16), g, NN)
            for block in range(rows // step):
                part = slice(block * step, (block + 1) * step)
                dk[block] = dk_now[part] if dk[block] is None else dk[block] + dk_now[part]
                dv[block] = dv_now[part] if dv[block] is None else dv[block] + dv_now[part]
            dq_ref[first : first + step, cols] = dot(k, score_grad, TN).T.astype(BF16)
        for block in range(size // step):
            part = slice(block * step, (block + 1) * step)
            dk_ref[part, cols] = dk[block].astype(BF16)
            dv_ref[part, cols] = dv[block].astype(BF16)
        if causal:
            doffs_ref[0, head : head + 1, :] = diagonal_sums(jnp.concatenate(spread, axis=1), size)


def pair_spec(size):
    return pl.BlockSpec((size, 2 * HEAD), lambda p, *_: (0, p))


def lane_spec(size):
    return pl.BlockSpec((1, 2, size), lambda p, *_: (p, 0, 0))


def attend_forward(lengths, offs, q, k, v):
    causal = offs is not None
    size = q.shape[0]
    pairs = HEADS // 2
    ins = [pair_spec(size)] * 3
    args = (q, k, v)
    if causal:
        ins = [lane_spec(size)] + ins
        args = (offs.reshape(pairs, 2, size),) + args
    return pl.pallas_call(
        functools.partial(forward_kernel, causal),
        out_shape=(
            jax.ShapeDtypeStruct(q.shape, BF16),
            jax.ShapeDtypeStruct((pairs, 2, size), F32),
        ),
        grid_spec=pltpu.PrefetchScalarGridSpec(
            num_scalar_prefetch=1,
            grid=(pairs,),
            in_specs=ins,
            out_specs=[pair_spec(size), lane_spec(size)],
        ),
        compiler_params=pltpu.CompilerParams(vmem_limit_bytes=VMEM),
        cost_estimate=pl.CostEstimate(
            flops=11 * 10**9, bytes_accessed=4 * 2**20, transcendentals=3 * 2**20
        ),
        name="attend_forward_self" if causal else "attend_forward_cross",
    )(lengths, *args)


def attend_backward(lengths, offs, q, k, v, g, lse):
    causal = offs is not None
    size = q.shape[0]
    pairs = HEADS // 2
    ins = [pair_spec(size)] * 4 + [lane_spec(size)]
    args = (q, k, v, g, lse)
    outs = [pair_spec(size)] * 3
    shapes = [jax.ShapeDtypeStruct(q.shape, BF16)] * 3
    if causal:
        ins = [lane_spec(size)] + ins
        args = (offs.reshape(pairs, 2, size),) + args
        outs = outs + [lane_spec(size)]
        shapes = shapes + [jax.ShapeDtypeStruct((pairs, 2, size), F32)]
    return pl.pallas_call(
        functools.partial(backward_kernel, causal),
        out_shape=tuple(shapes),
        grid_spec=pltpu.PrefetchScalarGridSpec(
            num_scalar_prefetch=1, grid=(pairs,), in_specs=ins, out_specs=outs
        ),
        compiler_params=pltpu.CompilerParams(vmem_limit_bytes=VMEM),
        cost_estimate=pl.CostEstimate(
            flops=17 * 10**9, bytes_accessed=6 * 2**20, transcendentals=3 * 2**20
        ),
        name="attend_backward_self" if causal else "attend_backward_cross",
    )(lengths, *args)


def after(array, *earlier):
    return lax.optimization_barrier((array,) + earlier)[0]


class Links:
    def __init__(self, reps, owners):
        self.owners = owners
        self.bits = owners.bit_length() - 1
        self.count = reps * owners
        self.rep = lax.axis_index("rep")
        self.owner = lax.axis_index("fsdp")
        self.core = self.rep % 2
        self.side = self.rep // 2
        self.core_word = self.core.reshape(1).astype(jnp.int32)

    def move(self, array, target):
        return lax.ppermute(
            array, ("rep", "fsdp"), [(device, target(device)) for device in range(self.count)]
        )

    def over_owner(self, array, bit):
        return self.move(array, lambda device: device ^ (1 << bit))

    def over_core(self, array):
        return self.move(array, lambda device: device ^ self.owners)

    def over_side(self, array):
        return self.move(array, lambda device: device ^ (2 * self.owners))

    def over_pair(self, array, first):
        def target(device):
            core = (device // self.owners) % 2
            return device ^ (1 if (core == 0) == first else 2 * self.owners)

        return self.move(array, target)

    def step(self, array, name):
        if name == "first":
            return self.over_pair(array, True)
        if name == "second":
            return self.over_pair(array, False)
        return self.over_owner(array, name)

    def far_to_near(self):
        return tuple(range(self.bits - 1, 0, -1))

    def places(self, core, order):
        index = jnp.arange(2 * self.owners)
        owner = jnp.full_like(index, self.owner)
        side = jnp.full_like(index, self.side)
        for at, name in enumerate(order):
            flip = (index >> at) & 1
            if name == "first":
                owner = owner ^ jnp.where(core == 0, flip, 0)
                side = side ^ jnp.where(core == 0, 0, flip)
            elif name == "second":
                owner = owner ^ jnp.where(core == 0, 0, flip)
                side = side ^ jnp.where(core == 0, flip, 0)
            else:
                owner = owner ^ (flip << name)
        return (owner * 2 + side).astype(jnp.int32)


def assemble_kernel(places, core, *refs):
    sources, out_ref, sems = refs[:4], refs[4], refs[5]
    width = sources[0].shape[-1]
    copies = []
    for half in range(2):
        column = core[0] if half == 0 else 1 - core[0]
        start = pl.multiple_of(column * width, width)
        for part in range(2):
            source = sources[2 * half + part]
            for index in range(source.shape[0]):
                at = part * source.shape[0] + index
                copies.append(
                    pltpu.make_async_copy(
                        source.at[index],
                        out_ref.at[:, places[half, at], :, pl.ds(start, width)],
                        sems.at[half, at],
                    )
                )
    for copy in copies:
        copy.start()
    for copy in copies:
        copy.wait()


def assemble(links, order, own, other):
    places = jnp.stack([links.places(links.core, order), links.places(1 - links.core, order)])
    half, weights, rows, columns = own[0].shape
    shape = (weights, 2 * half, rows, 2 * columns)
    out = pl.pallas_call(
        assemble_kernel,
        out_shape=jax.ShapeDtypeStruct(shape, BF16),
        grid_spec=pltpu.PrefetchScalarGridSpec(
            num_scalar_prefetch=2,
            grid=(1,),
            in_specs=[pl.BlockSpec(memory_space=pl.ANY)] * 4,
            out_specs=pl.BlockSpec(shape, lambda *_: (0, 0, 0, 0)),
            scratch_shapes=[pltpu.SemaphoreType.DMA((2, 2 * half))],
        ),
        compiler_params=pltpu.CompilerParams(vmem_limit_bytes=VMEM),
        name="assemble",
    )(places, links.core_word, *own, *other)
    return out.reshape(weights, 2 * half * rows, 2 * columns)


def own_block(links, shards):
    rows = shards[0].shape[0] // 2
    columns = shards[0].shape[1] // 2
    at = (links.side * rows, links.core * columns)
    return jnp.stack([lax.dynamic_slice(shard, at, (rows, columns)) for shard in shards])[None]


def gather_group(links, order, shards, earlier):
    block = own_block(links, shards)
    done = []
    parts = None
    for at, name in enumerate(order):
        if earlier:
            block = after(block, earlier[at])
        got = links.step(block, name)
        done.append(got)
        parts = [block, got]
        if at < len(order) - 1:
            block = jnp.concatenate(parts, axis=0)
    other = [links.over_core(part) for part in parts]
    return assemble(links, order, parts, other), done


def gather_small(links, values):
    block = values[None]
    for bit in range(links.bits):
        block = jnp.concatenate([block, links.over_owner(block, bit)], axis=0)
    return block[jnp.arange(links.owners) ^ links.owner]


def sum_small(links, values):
    values = values + links.over_core(values)
    values = values + links.over_side(values)
    for bit in range(links.bits):
        values = values + links.over_owner(values, bit)
    return values


def split_sum_kernel(picks, kept_one, kept_two, got_one, got_two, keep_ref, send_ref):
    keep_ref[0] = (kept_one[:, 0].astype(F32) + got_one[:, 0].astype(F32)).astype(BF16)
    send_ref[0] = (kept_two[:, 0].astype(F32) + got_two[:, 0].astype(F32)).astype(BF16)


def split_sum(picks, kept, got):
    weights, count, rows, columns = kept.shape
    half = count // 2
    keep = pl.BlockSpec((weights, 1, rows, columns), lambda i, picks: (0, picks[i], 0, 0))
    send = pl.BlockSpec((weights, 1, rows, columns), lambda i, picks: (0, picks[half + i], 0, 0))
    out = pl.BlockSpec((1, weights, rows, columns), lambda i, picks: (i, 0, 0, 0))
    return pl.pallas_call(
        split_sum_kernel,
        out_shape=(jax.ShapeDtypeStruct((half, weights, rows, columns), BF16),) * 2,
        grid_spec=pltpu.PrefetchScalarGridSpec(
            num_scalar_prefetch=1, grid=(half,), in_specs=[keep, send, keep, send], out_specs=[out, out]
        ),
        name="split_sum",
    )(picks, kept, kept, got, got)


def reduce_group(links, order, keep, send):
    weights, rows, columns = keep.shape
    shape = (weights, 2 * links.owners, rows // (2 * links.owners), columns)
    got = links.over_core(send).reshape(shape)
    keep = keep.reshape(shape)
    picks = links.places(links.core, order[::-1])
    keep, send = split_sum(picks, keep, got)
    for at, name in enumerate(order):
        got = links.step(send, name)
        if at < len(order) - 1:
            half = keep.shape[0] // 2
            send = (keep[half:].astype(F32) + got[half:].astype(F32)).astype(BF16)
            keep = (keep[:half].astype(F32) + got[:half].astype(F32)).astype(BF16)
    mine = (keep.astype(F32) + got.astype(F32)).astype(BF16)[0]
    got = links.over_side(mine)
    first = links.side == 0
    pair = jnp.concatenate([jnp.where(first, mine, got), jnp.where(first, got, mine)], axis=1)
    got = links.over_core(pair)
    first = links.core == 0
    pair = jnp.concatenate([jnp.where(first, pair, got), jnp.where(first, got, pair)], axis=2)
    return pair.astype(F32)


def matmul(a, b):
    return dot(a, b, NN)


def matmul_nt(a, b):
    return dot(a, b, NT)


def norm_forward(hidden, gain):
    scale = lax.rsqrt(jnp.mean(hidden * hidden, axis=-1, keepdims=True) + EPSILON)
    return (hidden * scale * gain, scale)


def norm_backward(hidden, scale, gain, upstream):
    gain_grad = jnp.sum(upstream * (hidden * scale), axis=0)
    weighted = upstream * gain
    inner = jnp.mean(weighted * hidden, axis=-1, keepdims=True)
    return (scale * weighted - hidden * (scale * scale * scale) * inner, gain_grad)


def smooth_gate(value):
    return jax.nn.gelu(value, approximate=True)


def weight_grads_kernel(count, other, core, *refs):
    rows, grads, out_ref = refs[:count], refs[count : 2 * count], refs[2 * count]
    column = 1 - core[0] if other else core[0]
    width = out_ref.shape[-1]
    start = pl.multiple_of(column * width, width)
    for at in range(count):
        out_ref[at] = dot(rows[at][...], grads[at][:, pl.ds(start, width)], TN).astype(BF16)


def weight_grads_half(links, other, rows, grads):
    count = len(rows)
    shape = (count, rows[0].shape[1], grads[0].shape[1] // 2)
    return pl.pallas_call(
        functools.partial(weight_grads_kernel, count, other),
        out_shape=jax.ShapeDtypeStruct(shape, BF16),
        grid_spec=pltpu.PrefetchScalarGridSpec(
            num_scalar_prefetch=1,
            grid=(1,),
            in_specs=[pl.BlockSpec(item.shape, lambda *_: (0, 0)) for item in (*rows, *grads)],
            out_specs=pl.BlockSpec(shape, lambda *_: (0, 0, 0)),
        ),
        compiler_params=pltpu.CompilerParams(vmem_limit_bytes=VMEM),
        cost_estimate=pl.CostEstimate(
            flops=2 * shape[0] * shape[1] * shape[2] * rows[0].shape[0],
            bytes_accessed=2 * shape[0] * shape[1] * shape[2],
            transcendentals=0,
        ),
        name="weight_grads",
    )(links.core_word, *rows, *grads)


def weight_grads(links, rows, grads):
    send = weight_grads_half(links, True, rows, grads)
    keep = weight_grads_half(links, False, rows, grads)
    return keep, send


def on_device(
    reps,
    owners,
    hidden_in,
    memory,
    lengths,
    buckets,
    cotangent,
    self_gain,
    self_query,
    self_key,
    self_value,
    self_out,
    bias_table,
    cross_gain,
    cross_query,
    cross_key,
    cross_value,
    cross_out,
    feed_gain,
    feed_gate,
    feed_up,
    feed_down,
):
    links = Links(reps, owners)
    width = hidden_in.shape[2]
    share = width // owners
    memory = memory[0]
    cotangent = cotangent[0]
    hidden = hidden_in[0].astype(F32)
    small = jnp.concatenate([self_gain, cross_gain, feed_gain, bias_table])
    small = gather_small(links, small).astype(F32)
    gain_one = small[:, :share].reshape(1, -1)
    gain_two = small[:, share : 2 * share].reshape(1, -1)
    gain_three = small[:, 2 * share : 3 * share].reshape(1, -1)
    table = small[:, 3 * share :].reshape(BUCKETS, HEADS)

    order = links.far_to_near() + ("first", "second")
    back = order[::-1]
    qkv, done = gather_group(links, order, (self_query, self_key, self_value), None)
    five, done = gather_group(
        links, order, (self_out, cross_query, cross_key, cross_value, cross_out), done
    )
    gate_up, done = gather_group(links, order, (feed_gate, feed_up), done)
    down, done = gather_group(links, order, (feed_down,), done)
    w_query, w_key, w_value = qkv
    w_out, w_cross_query, w_cross_key, w_cross_value, w_cross_out = five
    w_gate, w_up = gate_up
    w_down = down[0]

    picks = (buckets[:, None] == jnp.arange(BUCKETS)[None, :]).astype(F32)
    offsets = jnp.dot(picks, table, precision=PRECISE).T

    normed_one, scale_one = norm_forward(hidden, gain_one)
    normed_one = normed_one.astype(BF16)
    query = matmul(normed_one, w_query).astype(BF16)
    keys = matmul(normed_one, w_key).astype(BF16)
    values = matmul(normed_one, w_value).astype(BF16)
    mixed_one, lse_one = attend_forward(lengths, offsets, query, keys, values)
    after_self = hidden + matmul(mixed_one, w_out)
    normed_two, scale_two = norm_forward(after_self, gain_two)
    normed_two = normed_two.astype(BF16)
    cross_queries = matmul(normed_two, w_cross_query).astype(BF16)
    memory_keys = matmul(memory, w_cross_key).astype(BF16)
    memory_values = matmul(memory, w_cross_value).astype(BF16)
    mixed_two, lse_two = attend_forward(lengths, None, cross_queries, memory_keys, memory_values)
    after_cross = after_self + matmul(mixed_two, w_cross_out)
    normed_three, scale_three = norm_forward(after_cross, gain_three)
    normed_three = normed_three.astype(BF16)
    gate = matmul(normed_three, w_gate)
    lift = matmul(normed_three, w_up)
    activated, gate_back = jax.vjp(smooth_gate, gate)
    inner = (activated * lift).astype(BF16)
    layer_out = (after_cross + matmul(inner, w_down)).astype(BF16)

    down_sum = reduce_group(links, back, *weight_grads(links, [inner], [cotangent]))
    inner_grad = matmul_nt(cotangent, w_down)
    gate_grad = gate_back(inner_grad * lift)[0].astype(BF16)
    lift_grad = (inner_grad * activated).astype(BF16)
    gate_up_sum = reduce_group(
        links, back, *weight_grads(links, [normed_three] * 2, [gate_grad, lift_grad])
    )
    normed_grad = matmul_nt(gate_grad, w_gate) + matmul_nt(lift_grad, w_up)
    residual_grad, gain_three_grad = norm_backward(after_cross, scale_three, gain_three, normed_grad)
    carried = cotangent.astype(F32) + residual_grad

    branch_two = carried.astype(BF16)
    mixed_two_grad = matmul_nt(branch_two, w_cross_out).astype(BF16)
    cross_queries_grad, memory_keys_grad, memory_values_grad = attend_backward(
        lengths, None, cross_queries, memory_keys, memory_values, mixed_two_grad, lse_two
    )
    memory_grad = matmul_nt(memory_keys_grad, w_cross_key) + matmul_nt(
        memory_values_grad, w_cross_value
    )
    normed_grad = matmul_nt(cross_queries_grad, w_cross_query)
    residual_grad, gain_two_grad = norm_backward(after_self, scale_two, gain_two, normed_grad)
    carried = carried + residual_grad
    branch_one = carried.astype(BF16)
    five_sum = reduce_group(
        links,
        back,
        *weight_grads(
            links,
            [mixed_two, normed_two, memory, memory, mixed_one],
            [branch_two, cross_queries_grad, memory_keys_grad, memory_values_grad, branch_one],
        ),
    )

    mixed_one_grad = matmul_nt(branch_one, w_out).astype(BF16)
    query_grad, keys_grad, values_grad, offset_grad = attend_backward(
        lengths, offsets, query, keys, values, mixed_one_grad, lse_one
    )
    qkv_sum = reduce_group(
        links,
        back,
        *weight_grads(links, [normed_one] * 3, [query_grad, keys_grad, values_grad]),
    )
    normed_grad = (
        matmul_nt(query_grad, w_query)
        + matmul_nt(keys_grad, w_key)
        + matmul_nt(values_grad, w_value)
    )
    residual_grad, gain_one_grad = norm_backward(hidden, scale_one, gain_one, normed_grad)
    input_grad = carried + residual_grad
    table_grad = jnp.dot(picks.T, offset_grad.reshape(HEADS, -1).T, precision=PRECISE)

    small = jnp.concatenate(
        [
            gain_one_grad.reshape(owners, -1),
            gain_two_grad.reshape(owners, -1),
            gain_three_grad.reshape(owners, -1),
            table_grad.reshape(owners, -1),
        ],
        axis=1,
    )
    small = sum_small(links, small)
    small = lax.dynamic_index_in_dim(small, links.owner, 0, keepdims=False)
    return (
        layer_out[None],
        input_grad[None],
        memory_grad[None],
        small[:share],
        qkv_sum[0],
        qkv_sum[1],
        qkv_sum[2],
        five_sum[4],
        small[3 * share :],
        small[share : 2 * share],
        five_sum[1],
        five_sum[2],
        five_sum[3],
        five_sum[0],
        small[2 * share : 3 * share],
        gate_up_sum[0],
        gate_up_sum[1],
        down_sum[0],
    )


def solution(mesh):
    rows = P(("rep", "fsdp"), None, None)
    vector = P("fsdp")
    matrix = P("fsdp", None)
    attention = (vector,) + (matrix,) * 4
    return jax.shard_map(
        functools.partial(on_device, mesh.shape["rep"], mesh.shape["fsdp"]),
        mesh=mesh,
        in_specs=(rows, rows, P(("rep", "fsdp")), P(), rows)
        + attention
        + (vector,)
        + attention
        + (vector, matrix, matrix, matrix),
        out_specs=(rows, rows, rows)
        + attention
        + (vector,)
        + attention
        + (vector, matrix, matrix, matrix),
        check_vma=False,
    )
```

time: 2250 us -> 417 us (0.19); the launches traced: 2220 us -> 412 us
  waiting for transfers between devices: 1030 us -> 125 us
  local copies, waits for them, and re-layouts: 693 us -> 33 us
  matrix products: 285 us -> 42 us
  blocking collectives: 130 us -> 0 us
  Pallas kernels: 0 us -> 127 us
  starting transfers between devices: 1.5 us -> 57.3 us
  other arithmetic: 58.8 us -> 25 us
    reduce_scatter x13 -> x0, waiting for transfers between devices: 630 us -> none  [the longest x1 115 us: on_device(): lax.psum_scatter(gate_weight_grad, 'fsdp', scatter_dimension=0, tiled=True)]
    rev x18 -> x0, local copies, waits for them, and re-layouts: 277 us -> none  [the longest x12 182 us: toeplitz(): return spread[:, :, length - 1::-1]]
    dot_general x119 -> x24, matrix products: 285 us -> 42 us  [the longest x22 41.7 us: dot(): return lax.dot_general(a, b, dims, preferred_element_type=F32)]
    unnamed x42 -> x0, waiting for transfers between devices: 213 us -> none
    all_gather x11 -> x0, waiting for transfers between devices: 190 us -> none  [the longest x1 55.3 us: gather_feed(): lax.all_gather(feed_down, 'fsdp', axis=0, tiled=True)]
    reshape x22 -> x6, local copies, waits for them, and re-layouts: 175 us -> 0.38 us  [the longest x1 0.08 us: on_device(): table = small[:, 3 * share:].reshape(BUCKETS, HEADS)]
    pallas_call x0 -> x20, Pallas kernels: none -> 127 us  [the longest x2 31.3 us: attend_backward(): pl.pallas_call(functools.partial(backward_kernel, causal), out_shape=tupl...]
    ppermute x0 -> x60, waiting for transfers between devices: none -> 125 us  [move(): lax.ppermute(array, ('rep', 'fsdp'), [(device, target(device)) for device...]
  transfers between devices with their start and end apart: 33 -> 60, of which waited for: 23 -> 24; matrix products, arithmetic and copies ran while one was open for 42% -> 16% of each run, Pallas kernels for 0% -> 22%
where the time goes in v1:
time: 417 us; the launch traced here: 412 us
  Pallas kernels  127 us (30%)
  waiting for transfers between devices  125 us (30%)
  starting transfers between devices  57.3 us (14%)
  matrix products  42 us (10%)
  local copies, waits for them, and re-layouts  33 us (8%)
  other arithmetic  25 us (6%)
    ppermute x60, waiting for transfers between devices, move(): lax.ppermute(array, ('rep', 'fsdp'), [(device, target(device)) for device...  125 us
    ppermute x60, starting transfers between devices, move(): lax.ppermute(array, ('rep', 'fsdp'), [(device, target(device)) for device...  57.3 us
    dot_general x22, matrix products, dot(): return lax.dot_general(a, b, dims, preferred_element_type=F32)  41.7 us
    pallas_call x2, Pallas kernels, attend_backward(): pl.pallas_call(functools.partial(backward_kernel, causal), out_shape=tupl...  31.3 us
    pallas_call x4, Pallas kernels, split_sum(): pl.pallas_call(split_sum_kernel, out_shape=(jax.ShapeDtypeStruct((half, w...  29 us
    pallas_call x8, Pallas kernels, weight_grads_half(): pl.pallas_call(functools.partial(weight_grads_kernel, count, other), out_...  25.4 us
    pallas_call x2, Pallas kernels, attend_forward(): pl.pallas_call(functools.partial(forward_kernel, causal), out_shape=(jax....  22.6 us
    pallas_call x4, Pallas kernels, assemble(): pl.pallas_call(assemble_kernel, out_shape=jax.ShapeDtypeStruct(shape, BF1...  18.9 us
  transfers between devices with their start and end apart: 60, of which 24 were waited for; matrix products, arithmetic and copies ran while one was open for 16% of the time, Pallas kernels for 22%

profile of v1, /device:TPU:0, one launch (start us, length us, event | category | flops | bytes accessed | tf_op | source)
XLA Modules:
  0.0 411.8 jit_solution(6460759818166211037)
XLA Ops:
  18.1 7.5 %collective-permute-done.4 = bf16[2,3,48,384]{3,2,1,0:T(8,128)(2,1)S(1)} collective-permute-done((bf16[2,3,48,384]{3,2,1,0:T(8,128)(2,1)S(1)}, bf16[2,3,48,384]{3,2,1,0:T(8,128)(2,1)S(1)}, u32[]{:S(2)}, u32[]{:S(2)}) %collective-permute-start.4) | collective-permute-done | bytes 221216 | tf_op jit(solution)/shard_map/ppermute | solution.py:217
  35.7 4.2 %collective-permute-done.10 = bf16[2,5,48,384]{3,2,1,0:T(8,128)(2,1)S(1)} collective-permute-done((bf16[2,5,48,384]{3,2,1,0:T(8,128)(2,1)S(1)}, bf16[2,5,48,384]{3,2,1,0:T(8,128)(2,1)S(1)}, u32[]{:S(2)}, u32[]{:S(2)}) %collective-permute-start.10) | collective-permute-done | bytes 368672 | tf_op jit(solution)/shard_map/ppermute | solution.py:217
  62.7 4.4 %collective-permute-done.22 = bf16[2,1,128,384]{3,2,1,0:T(8,128)(2,1)} collective-permute-done((bf16[2,1,128,384]{3,2,1,0:T(8,128)(2,1)S(1)}, bf16[2,1,128,384]{3,2,1,0:T(8,128)(2,1)}, u32[]{:S(2)}, u32[]{:S(2)}) %collective-permute-start.22) | collective-permute-done | bytes 196640 | tf_op jit(solution)/shard_map/ppermute | solution.py:217
  68.2 5.4 %collective-permute-done.17 = bf16[4,2,48,1024]{3,2,1,0:T(8,128)(2,1)} collective-permute-done((bf16[4,2,48,1024]{3,2,1,0:T(8,128)(2,1)S(1)}, bf16[4,2,48,1024]{3,2,1,0:T(8,128)(2,1)}, u32[]{:S(2)}, u32[]{:S(2)}) %collective-permute-start.17) | collective-permute-done | bytes 786464 | tf_op jit(solution)/shard_map/ppermute | solution.py:217
  74.9 4.8 %assemble.4 = bf16[3,16,48,768]{3,2,1,0:T(8,128)(2,1)} custom-call(s32[2,16]{1,0:T(2,128)S(1)} %pad_add_fusion.places, s32[1]{0:T(128)} %bitcast.5.core, bf16[8,3,48,384]{3,2,1,0:T(8,128)(2,1)S(1)} %pad_maximum_fusion.2.refs_0_, bf16[8,3,48,384]{3,2,1,0:T(8,128)(2,1)} %collective-permute-done.6.refs_1_, ...), custom_call_target="tpu_custom_call" | custom-call | tf_op jit(solution)/shard_map/assemble/pallas_call | solution.py:292
  88.8 10.2 %attend_forward_self.1 = (bf16[512,768]{1,0:T(8,128)(2,1)S(1)}, f32[6,2,512]{2,1,0:T(2,128)S(1)}) custom-call(s32[1]{0:T(128)S(6)} %copy.61.lengths, f32[6,2,512]{2,1,0:T(2,128)S(1)} %copy.45.refs_0_, bf16[512,768]{1,0:T(8,128)(2,1)S(1)} %convolution_convert_fusion.7.refs_1_, bf16[512,768]{1,0:T(8,128)(2,1)S(1)} %convolution_convert_fusion.6.refs_2_, ...), custom_call_target="tpu_custom_call" | custom-call | flops 11000000512 | bytes 4194304 | tf_op jit(solution)/shard_map/attend_forward_self/pallas_call | solution.py:154
  100.1 5.0 %assemble.5 = bf16[5,16,48,768]{3,2,1,0:T(8,128)(2,1)} custom-call(s32[2,16]{1,0:T(2,128)S(1)} %pad_add_fusion.places, s32[1]{0:T(128)} %bitcast.5.core, bf16[8,5,48,384]{3,2,1,0:T(8,128)(2,1)S(1)} %pad_maximum_fusion.1.refs_0_, bf16[8,5,48,384]{3,2,1,0:T(8,128)(2,1)} %collective-permute-done.12.refs_1_, ...), custom_call_target="tpu_custom_call" | custom-call | tf_op jit(solution)/shard_map/assemble/pallas_call | solution.py:292
  105.1 4.1 fusion.66
  114.4 5.2 %collective-permute-done.18.refs_1_ = bf16[8,2,48,1024]{3,2,1,0:T(8,128)(2,1)S(1)} collective-permute-done((bf16[8,2,48,1024]{3,2,1,0:T(8,128)(2,1)S(1)}, bf16[8,2,48,1024]{3,2,1,0:T(8,128)(2,1)S(1)}, u32[]{:S(2)}, u32[]{:S(2)}) %collective-permute-start.18) | collective-permute-done | bytes 1572896 | tf_op jit(solution)/shard_map/ppermute | solution.py:217
  119.7 12.3 %attend_forward_cross.1 = (bf16[512,768]{1,0:T(8,128)(2,1)S(1)}, f32[6,2,512]{2,1,0:T(2,128)S(1)}) custom-call(s32[1]{0:T(128)S(6)} %copy.61.lengths, bf16[512,768]{1,0:T(8,128)(2,1)S(1)} %convolution_convert_fusion.4.refs_0_, bf16[512,768]{1,0:T(8,128)(2,1)S(1)} %fusion.25.refs_1_, bf16[512,768]{1,0:T(8,128)(2,1)S(1)} %fusion.26.refs_2_), custom_call_target="tpu_custom_call" | custom-call | flops 11000000512 | bytes 4194304 | tf_op jit(solution)/shard_map/attend_forward_cross/pallas_call | solution.py:154
  134.1 9.9 %collective-permute-done.24.refs_1_ = bf16[8,1,128,384]{3,2,1,0:T(8,128)(2,1)S(1)} collective-permute-done((bf16[8,1,128,384]{3,2,1,0:T(8,128)(2,1)S(1)}, bf16[8,1,128,384]{3,2,1,0:T(8,128)(2,1)S(1)}, u32[]{:S(2)}, u32[]{:S(2)}) %collective-permute-start.24) | collective-permute-done | bytes 786464 | tf_op jit(solution)/shard_map/ppermute | solution.py:217
  144.1 6.1 %assemble.6 = bf16[2,16,48,2048]{3,2,1,0:T(8,128)(2,1)} custom-call(s32[2,16]{1,0:T(2,128)S(1)} %pad_add_fusion.places, s32[1]{0:T(128)} %bitcast.5.core, bf16[8,2,48,1024]{3,2,1,0:T(8,128)(2,1)S(1)} %pad_maximum_fusion.refs_0_, bf16[8,2,48,1024]{3,2,1,0:T(8,128)(2,1)S(1)} %collective-permute-done.18.refs_1_, ...), custom_call_target="tpu_custom_call" | custom-call | tf_op jit(solution)/shard_map/assemble/pallas_call | solution.py:292
  150.2 5.6 %fusion.65 = (bf16[1,16,48,2048]{3,2,1,0:T(8,128)(2,1)}, bf16[1,16,48,2048]{3,2,1,0:T(8,128)(2,1)S(1)}) fusion(bf16[2,16,48,2048]{3,2,1,0:T(8,128)(2,1)} %assemble.6), kind=kLoop, calls=%fused_computation.220 | loop fusion | bytes 12582912 | tf_op jit(solution)/shard_map/unstack | solution.py:498
  166.8 6.2 %fusion.6 = (bf16[512,2048]{1,0:T(8,128)(2,1)S(1)}, bf16[512,2048]{1,0:T(8,128)(2,1)S(1)}, bf16[512,2048]{1,0:T(8,128)(2,1)}) fusion(f32[512,2048]{1,0:T(8,128)S(1)} %copy-done.80, f32[2048,512]{0,1:T(8,128)S(1)} %fusion.56, bf16[512,768]{1,0:T(8,128)(2,1)S(1)} %multiply_convert_fusion.1.refs_0_.refs_1_, bf16[768,2048]{1,0:T(8,128)(2,1)S(1)} %bitcast.218), kind=kOutput, calls=%fused_computation.9 | convolution fusion | flops 1637875712 | bytes 18612224 | tf_op jit(solution)/shard_map/dot_general | solution.py:25
  178.6 15.0 %attend_backward_cross.1 = (bf16[512,768]{1,0:T(8,128)(2,1)S(1)}, bf16[512,768]{1,0:T(8,128)(2,1)S(1)}, bf16[512,768]{1,0:T(8,128)(2,1)S(1)}) custom-call(s32[1]{0:T(128)S(6)} %copy.61.lengths, bf16[512,768]{1,0:T(8,128)(2,1)S(1)} %convolution_convert_fusion.4.refs_0_, bf16[512,768]{1,0:T(8,128)(2,1)S(1)} %fusion.25.refs_1_, ...), custom_call_target="tpu_custom_call" | custom-call | flops 16999999488 | bytes 6291456 | tf_op jit(solution)/shard_map/attend_backward_cross/pallas_call | solution.py:187
  198.4 16.3 %attend_backward_self.1 = (bf16[512,768]{1,0:T(8,128)(2,1)S(1)}, bf16[512,768]{1,0:T(8,128)(2,1)S(1)}, bf16[512,768]{1,0:T(8,128)(2,1)S(1)}, f32[6,2,512]{2,1,0:T(2,128)S(1)}) custom-call(s32[1]{0:T(128)S(6)} %copy.61.lengths, f32[6,2,512]{2,1,0:T(2,128)S(1)} %copy.45.refs_0_, bf16[512,768]{1,0:T(8,128)(2,1)S(1)} %copy-done.43, ...), custom_call_target="tpu_custom_call" | custom-call | flops 16999999488 | bytes 6291456 | tf_op jit(solution)/shard_map/attend_backward_self/pallas_call | solution.py:187
  227.6 4.0 fusion.16
  235.6 5.3 %weight_grads.11 = bf16[5,768,384]{2,1,0:T(8,128)(2,1)} custom-call(s32[1]{0:T(128)} %bitcast.5.core, bf16[512,768]{1,0:T(8,128)(2,1)S(1)} %copy-done.18, bf16[512,768]{1,0:T(8,128)(2,1)S(1)} %copy-done.24, bf16[512,768]{1,0:T(8,128)(2,1)S(1)} %bitcast.200, bf16[512,768]{1,0:T(8,128)(2,1)S(1)} %bitcast.201, bf16[512,768]{1,0:T(8,128)(2,1)S(1)} %copy-done.36, ...), custom_call_target="tpu_custom_call" | custom-call | flops 1509949440 | bytes 2949120 | tf_op jit(solution)/shard_map/weight_grads/pallas_call | solution.py:426
  249.6 6.8 %split_sum.7 = (bf16[8,1,128,384]{3,2,1,0:T(8,128)(2,1)}, bf16[8,1,128,384]{3,2,1,0:T(8,128)(2,1)}) custom-call(s32[16]{0:T(128)} %fusion.54.picks, bf16[1,16,128,384]{3,2,1,0:T(8,128)(2,1)} %bitcast.198, bf16[1,16,128,384]{3,2,1,0:T(8,128)(2,1)} %bitcast.199, bf16[1,16,128,384]{3,2,1,0:T(8,128)(2,1)} %bitcast.63.got_one.got_two, ...), custom_call_target="tpu_custom_call" | custom-call | tf_op jit(solution)/shard_map/split_sum/pallas_call | solution.py:357
  262.9 6.0 %collective-permute-done.28 = f32[8,336]{1,0:T(8,128)S(1)} collective-permute-done((f32[8,336]{1,0:T(8,128)S(1)}, f32[8,336]{1,0:T(8,128)S(1)}, u32[]{:S(2)}, u32[]{:S(2)}) %collective-permute-start.28) | collective-permute-done | bytes 10784 | tf_op jit(solution)/shard_map/ppermute | solution.py:217
  280.3 6.8 %split_sum.4 = (bf16[8,3,48,384]{3,2,1,0:T(8,128)(2,1)}, bf16[8,3,48,384]{3,2,1,0:T(8,128)(2,1)}) custom-call(s32[16]{0:T(128)} %fusion.54.picks, bf16[3,16,48,384]{3,2,1,0:T(8,128)(2,1)} %bitcast.196, bf16[3,16,48,384]{3,2,1,0:T(8,128)(2,1)} %bitcast.197, bf16[3,16,48,384]{3,2,1,0:T(8,128)(2,1)} %bitcast.41.got_one.got_two, ...), custom_call_target="tpu_custom_call" | custom-call | tf_op jit(solution)/shard_map/split_sum/pallas_call | solution.py:357
  292.1 5.2 %weight_grads.10 = bf16[5,768,384]{2,1,0:T(8,128)(2,1)} custom-call(s32[1]{0:T(128)} %bitcast.5.core, bf16[512,768]{1,0:T(8,128)(2,1)S(1)} %copy-done.19, bf16[512,768]{1,0:T(8,128)(2,1)S(1)} %copy-done.25, bf16[512,768]{1,0:T(8,128)(2,1)S(1)} %bitcast.202, bf16[512,768]{1,0:T(8,128)(2,1)S(1)} %bitcast.203, bf16[512,768]{1,0:T(8,128)(2,1)S(1)} %copy-done.37, ...), custom_call_target="tpu_custom_call" | custom-call | flops 1509949440 | bytes 2949120 | tf_op jit(solution)/shard_map/weight_grads/pallas_call | solution.py:426
  306.4 7.4 %split_sum.5 = (bf16[8,5,48,384]{3,2,1,0:T(8,128)(2,1)}, bf16[8,5,48,384]{3,2,1,0:T(8,128)(2,1)}) custom-call(s32[16]{0:T(128)} %fusion.54.picks, bf16[5,16,48,384]{3,2,1,0:T(8,128)(2,1)} %bitcast.208, bf16[5,16,48,384]{3,2,1,0:T(8,128)(2,1)} %bitcast.209, bf16[5,16,48,384]{3,2,1,0:T(8,128)(2,1)} %bitcast.47.got_one.got_two, ...), custom_call_target="tpu_custom_call" | custom-call | tf_op jit(solution)/shard_map/split_sum/pallas_call | solution.py:357
  316.2 4.9 %collective-permute-done.57 = bf16[1,1,128,384]{3,2,1,0:T(8,128)(2,1)S(1)} collective-permute-done((bf16[1,1,128,384]{3,2,1,0:T(8,128)(2,1)S(1)}, bf16[1,1,128,384]{3,2,1,0:T(8,128)(2,1)S(1)}, u32[]{:S(2)}, u32[]{:S(2)}) %collective-permute-start.57) | collective-permute-done | bytes 98336 | tf_op jit(solution)/shard_map/ppermute | solution.py:217
  325.0 7.9 %split_sum.6 = (bf16[8,2,48,1024]{3,2,1,0:T(8,128)(2,1)}, bf16[8,2,48,1024]{3,2,1,0:T(8,128)(2,1)}) custom-call(s32[16]{0:T(128)} %fusion.54.picks, bf16[2,16,48,1024]{3,2,1,0:T(8,128)(2,1)} %bitcast.206, bf16[2,16,48,1024]{3,2,1,0:T(8,128)(2,1)} %bitcast.207, bf16[2,16,48,1024]{3,2,1,0:T(8,128)(2,1)} %bitcast.58.got_one.got_two, ...), custom_call_target="tpu_custom_call" | custom-call | tf_op jit(solution)/shard_map/split_sum/pallas_call | solution.py:357
  337.2 7.3 %collective-permute-done.36 = bf16[1,3,48,384]{3,2,1,0:T(8,128)(2,1)S(1)} collective-permute-done((bf16[1,3,48,384]{3,2,1,0:T(8,128)(2,1)S(1)}, bf16[1,3,48,384]{3,2,1,0:T(8,128)(2,1)S(1)}, u32[]{:S(2)}, u32[]{:S(2)}) %collective-permute-start.36) | collective-permute-done | bytes 110624 | tf_op jit(solution)/shard_map/ppermute | solution.py:217
  348.0 17.1 %collective-permute-done.37 = bf16[3,48,384]{2,1,0:T(8,128)(2,1)S(1)} collective-permute-done((bf16[3,48,384]{2,1,0:T(8,128)(2,1)S(1)}, bf16[3,48,384]{2,1,0:T(8,128)(2,1)S(1)}, u32[]{:S(2)}, u32[]{:S(2)}) %collective-permute-start.37) | collective-permute-done | bytes 110624 | tf_op jit(solution)/shard_map/ppermute | solution.py:217
  366.3 8.6 %collective-permute-done.42 = bf16[2,5,48,384]{3,2,1,0:T(8,128)(2,1)S(1)} collective-permute-done((bf16[2,5,48,384]{3,2,1,0:T(8,128)(2,1)S(1)}, bf16[2,5,48,384]{3,2,1,0:T(8,128)(2,1)S(1)}, u32[]{:S(2)}, u32[]{:S(2)}) %collective-permute-start.42) | collective-permute-done | bytes 368672 | tf_op jit(solution)/shard_map/ppermute | solution.py:217
  375.1 8.1 %collective-permute-done.43 = bf16[1,5,48,384]{3,2,1,0:T(8,128)(2,1)S(1)} collective-permute-done((bf16[1,5,48,384]{3,2,1,0:T(8,128)(2,1)S(1)}, bf16[1,5,48,384]{3,2,1,0:T(8,128)(2,1)S(1)}, u32[]{:S(2)}, u32[]{:S(2)}) %collective-permute-start.43) | collective-permute-done | bytes 184352 | tf_op jit(solution)/shard_map/ppermute | solution.py:217
  389.1 4.4 %collective-permute-done.49 = bf16[2,2,48,1024]{3,2,1,0:T(8,128)(2,1)S(1)} collective-permute-done((bf16[2,2,48,1024]{3,2,1,0:T(8,128)(2,1)S(1)}, bf16[2,2,48,1024]{3,2,1,0:T(8,128)(2,1)S(1)}, u32[]{:S(2)}, u32[]{:S(2)}) %collective-permute-start.49) | collective-permute-done | bytes 393248 | tf_op jit(solution)/shard_map/ppermute | solution.py:217
  394.5 7.7 %collective-permute-done.50 = bf16[1,2,48,1024]{3,2,1,0:T(8,128)(2,1)S(1)} collective-permute-done((bf16[1,2,48,1024]{3,2,1,0:T(8,128)(2,1)S(1)}, bf16[1,2,48,1024]{3,2,1,0:T(8,128)(2,1)S(1)}, u32[]{:S(2)}, u32[]{:S(2)}) %collective-permute-start.50) | collective-permute-done | bytes 196640 | tf_op jit(solution)/shard_map/ppermute | solution.py:217
  403.6 4.4 %collective-permute-done.51 = bf16[2,48,1024]{2,1,0:T(8,128)(2,1)S(1)} collective-permute-done((bf16[2,48,1024]{2,1,0:T(8,128)(2,1)S(1)}, bf16[2,48,1024]{2,1,0:T(8,128)(2,1)S(1)}, u32[]{:S(2)}, u32[]{:S(2)}) %collective-permute-start.51) | collective-permute-done | bytes 196640 | tf_op jit(solution)/shard_map/ppermute | solution.py:217
  (400 shorter events, 174.6 us)
Async XLA Ops:
  1.5 39.2 %collective-permute-start = (bf16[1,336]{1,0:T(2,128)(2,1)S(1)}, bf16[1,336]{1,0:T(2,128)(2,1)S(1)}, u32[]{:S(2)}, u32[]{:S(2)}) collective-permute-start(bf16[1,336]{1,0:T(2,128)(2,1)S(1)} %broadcast_in_dim.112), channel_id=1, source_target_pairs={{0,1},{1,0},{2,3},{3,2},{4,5},{5,4},{6,7},{7,6},{8,9},{9,8},{10,11... | collective-permute-start | bytes 2024 | tf_op jit(solution)/shard_map/ppermute | solution.py:217
  34.2 21.5 %collective-permute-start.6 = (bf16[8,3,48,384]{3,2,1,0:T(8,128)(2,1)S(1)}, bf16[8,3,48,384]{3,2,1,0:T(8,128)(2,1)}, u32[]{:S(2)}, u32[]{:S(2)}) collective-permute-start(bf16[8,3,48,384]{3,2,1,0:T(8,128)(2,1)S(1)} %pad_maximum_fusion.2.refs_0_), channel_id=1, source_target_pairs={{0,16},{1,17},{2,18},{3,19},{4,20},{5,21},{6,22},{7,23},{8,9},{9,8... | collective-permute-start | bytes 2654216 | tf_op jit(solution)/shard_map/ppermute | solution.py:217
  40.1 15.0 %collective-permute-start.11 = (bf16[4,5,48,384]{3,2,1,0:T(8,128)(2,1)S(1)}, bf16[4,5,48,384]{3,2,1,0:T(8,128)(2,1)}, u32[]{:S(2)}, u32[]{:S(2)}) collective-permute-start(bf16[4,5,48,384]{3,2,1,0:T(8,128)(2,1)S(1)} %pad_maximum_fusion.5), channel_id=1, source_target_pairs={{0,1},{1,0},{2,3},{3,2},{4,5},{5,4},{6,7},{7,6},{8,24},{9,25},{10,... | collective-permute-start | bytes 2211848 | tf_op jit(solution)/shard_map/ppermute | solution.py:217
  40.8 13.1 %collective-permute-start.16 = (bf16[2,2,48,1024]{3,2,1,0:T(8,128)(2,1)S(1)}, bf16[2,2,48,1024]{3,2,1,0:T(8,128)(2,1)}, u32[]{:S(2)}, u32[]{:S(2)}) collective-permute-start(bf16[2,2,48,1024]{3,2,1,0:T(8,128)(2,1)S(1)} %pad_maximum_fusion.7), channel_id=1, source_target_pairs={{0,2},{1,3},{2,0},{3,1},{4,6},{5,7},{6,4},{7,5},{8,10},{9,11},{10,... | collective-permute-start | bytes 1179656 | tf_op jit(solution)/shard_map/ppermute | solution.py:217
  54.0 20.9 %collective-permute-start.7 = (bf16[8,3,48,384]{3,2,1,0:T(8,128)(2,1)S(1)}, bf16[8,3,48,384]{3,2,1,0:T(8,128)(2,1)}, u32[]{:S(2)}, u32[]{:S(2)}) collective-permute-start(bf16[8,3,48,384]{3,2,1,0:T(8,128)(2,1)S(1)} %pad_maximum_fusion.2.refs_0_), channel_id=1, source_target_pairs={{0,8},{1,9},{2,10},{3,11},{4,12},{5,13},{6,14},{7,15},{8,0},{9,1},... | collective-permute-start | bytes 2654216 | tf_op jit(solution)/shard_map/ppermute | solution.py:217
  55.1 18.5 %collective-permute-start.17 = (bf16[4,2,48,1024]{3,2,1,0:T(8,128)(2,1)S(1)}, bf16[4,2,48,1024]{3,2,1,0:T(8,128)(2,1)}, u32[]{:S(2)}, u32[]{:S(2)}) collective-permute-start(bf16[4,2,48,1024]{3,2,1,0:T(8,128)(2,1)S(1)} %pad_maximum_fusion.3), channel_id=1, source_target_pairs={{0,1},{1,0},{2,3},{3,2},{4,5},{5,4},{6,7},{7,6},{8,24},{9,25},{10,... | collective-permute-start | bytes 2359304 | tf_op jit(solution)/shard_map/ppermute | solution.py:217
  55.6 19.3 %collective-permute-start.8 = (bf16[8,3,48,384]{3,2,1,0:T(8,128)(2,1)}, bf16[8,3,48,384]{3,2,1,0:T(8,128)(2,1)}, u32[]{:S(2)}, u32[]{:S(2)}) collective-permute-start(bf16[8,3,48,384]{3,2,1,0:T(8,128)(2,1)} %collective-permute-done.6.refs_1_), channel_id=1, source_target_pairs={{0,8},{1,9},{2,10},{3,11},{4,12},{5,13},{6,14},{7,15},{8,0},{9,1},... | collective-permute-start | bytes 2654216 | tf_op jit(solution)/shard_map/ppermute | solution.py:217
  58.0 28.8 %collective-permute-start.12 = (bf16[8,5,48,384]{3,2,1,0:T(8,128)(2,1)S(1)}, bf16[8,5,48,384]{3,2,1,0:T(8,128)(2,1)}, u32[]{:S(2)}, u32[]{:S(2)}) collective-permute-start(bf16[8,5,48,384]{3,2,1,0:T(8,128)(2,1)S(1)} %pad_maximum_fusion.1.refs_0_), channel_id=1, source_target_pairs={{0,16},{1,17},{2,18},{3,19},{4,20},{5,21},{6,22},{7,23},{8,9},{9,8... | collective-permute-start | bytes 4423688 | tf_op jit(solution)/shard_map/ppermute | solution.py:217
  68.1 32.0 %collective-permute-start.13 = (bf16[8,5,48,384]{3,2,1,0:T(8,128)(2,1)S(1)}, bf16[8,5,48,384]{3,2,1,0:T(8,128)(2,1)S(1)}, u32[]{:S(2)}, u32[]{:S(2)}) collective-permute-start(bf16[8,5,48,384]{3,2,1,0:T(8,128)(2,1)S(1)} %pad_maximum_fusion.1.refs_0_), channel_id=1, source_target_pairs={{0,8},{1,9},{2,10},{3,11},{4,12},{5,13},{6,14},{7,15},{8,0},{9,1},... | collective-permute-start | bytes 4423688 | tf_op jit(solution)/shard_map/ppermute | solution.py:217
  73.6 25.5 %collective-permute-start.23 = (bf16[4,1,128,384]{3,2,1,0:T(8,128)(2,1)S(1)}, bf16[4,1,128,384]{3,2,1,0:T(8,128)(2,1)S(1)}, u32[]{:S(2)}, u32[]{:S(2)}) collective-permute-start(bf16[4,1,128,384]{3,2,1,0:T(8,128)(2,1)S(1)} %pad_maximum_fusion.8), channel_id=1, source_target_pairs={{0,1},{1,0},{2,3},{3,2},{4,5},{5,4},{6,7},{7,6},{8,24},{9,25},{10,... | collective-permute-start | bytes 1179656 | tf_op jit(solution)/shard_map/ppermute | solution.py:217
  86.8 13.3 %collective-permute-start.14 = (bf16[8,5,48,384]{3,2,1,0:T(8,128)(2,1)}, bf16[8,5,48,384]{3,2,1,0:T(8,128)(2,1)S(1)}, u32[]{:S(2)}, u32[]{:S(2)}) collective-permute-start(bf16[8,5,48,384]{3,2,1,0:T(8,128)(2,1)} %collective-permute-done.12.refs_1_), channel_id=1, source_target_pairs={{0,8},{1,9},{2,10},{3,11},{4,12},{5,13},{6,14},{7,15},{8,0},{9,1},... | collective-permute-start | bytes 4423688 | tf_op jit(solution)/shard_map/ppermute | solution.py:217
  99.2 20.5 %collective-permute-start.18 = (bf16[8,2,48,1024]{3,2,1,0:T(8,128)(2,1)S(1)}, bf16[8,2,48,1024]{3,2,1,0:T(8,128)(2,1)S(1)}, u32[]{:S(2)}, u32[]{:S(2)}) collective-permute-start(bf16[8,2,48,1024]{3,2,1,0:T(8,128)(2,1)S(1)} %pad_maximum_fusion.refs_0_), channel_id=1, source_target_pairs={{0,16},{1,17},{2,18},{3,19},{4,20},{5,21},{6,22},{7,23},{8,9},{9,8... | collective-permute-start | bytes 4718600 | tf_op jit(solution)/shard_map/ppermute | solution.py:217
  100.1 44.0 %collective-permute-start.19 = (bf16[8,2,48,1024]{3,2,1,0:T(8,128)(2,1)S(1)}, bf16[8,2,48,1024]{3,2,1,0:T(8,128)(2,1)S(1)}, u32[]{:S(2)}, u32[]{:S(2)}) collective-permute-start(bf16[8,2,48,1024]{3,2,1,0:T(8,128)(2,1)S(1)} %pad_maximum_fusion.refs_0_), channel_id=1, source_target_pairs={{0,8},{1,9},{2,10},{3,11},{4,12},{5,13},{6,14},{7,15},{8,0},{9,1},... | collective-permute-start | bytes 4718600 | tf_op jit(solution)/shard_map/ppermute | solution.py:217
  119.7 24.4 %collective-permute-start.20 = (bf16[8,2,48,1024]{3,2,1,0:T(8,128)(2,1)S(1)}, bf16[8,2,48,1024]{3,2,1,0:T(8,128)(2,1)}, u32[]{:S(2)}, u32[]{:S(2)}) collective-permute-start(bf16[8,2,48,1024]{3,2,1,0:T(8,128)(2,1)S(1)} %collective-permute-done.18.refs_1_), channel_id=1, source_target_pairs={{0,8},{1,9},{2,10},{3,11},{4,12},{5,13},{6,14},{7,15},{8,0},{9,1},... | collective-permute-start | bytes 4718600 | tf_op jit(solution)/shard_map/ppermute | solution.py:217
  134.0 25.6 %collective-permute-start.25 = (bf16[8,1,128,384]{3,2,1,0:T(8,128)(2,1)S(1)}, bf16[8,1,128,384]{3,2,1,0:T(8,128)(2,1)S(1)}, u32[]{:S(2)}, u32[]{:S(2)}) collective-permute-start(bf16[8,1,128,384]{3,2,1,0:T(8,128)(2,1)S(1)} %pad_maximum_fusion.4.refs_0_), channel_id=1, source_target_pairs={{0,8},{1,9},{2,10},{3,11},{4,12},{5,13},{6,14},{7,15},{8,0},{9,1},... | collective-permute-start | bytes 2359304 | tf_op jit(solution)/shard_map/ppermute | solution.py:217
  144.1 15.6 %collective-permute-start.26 = (bf16[8,1,128,384]{3,2,1,0:T(8,128)(2,1)S(1)}, bf16[8,1,128,384]{3,2,1,0:T(8,128)(2,1)S(1)}, u32[]{:S(2)}, u32[]{:S(2)}) collective-permute-start(bf16[8,1,128,384]{3,2,1,0:T(8,128)(2,1)S(1)} %collective-permute-done.24.refs_1_), channel_id=1, source_target_pairs={{0,8},{1,9},{2,10},{3,11},{4,12},{5,13},{6,14},{7,15},{8,0},{9,1},... | collective-permute-start | bytes 2359304 | tf_op jit(solution)/shard_map/ppermute | solution.py:217
  223.2 26.4 %collective-permute-start.53 = (bf16[1,2048,384]{2,1,0:T(8,128)(2,1)}, bf16[1,2048,384]{2,1,0:T(8,128)(2,1)}, u32[]{:S(2)}, u32[]{:S(2)}) collective-permute-start(bf16[1,2048,384]{2,1,0:T(8,128)(2,1)} %weight_grads.15), channel_id=1, source_target_pairs={{0,8},{1,9},{2,10},{3,11},{4,12},{5,13},{6,14},{7,15},{8,0},{9,1},... | collective-permute-start | bytes 4718600 | tf_op jit(solution)/shard_map/ppermute | solution.py:217
  234.4 45.9 %collective-permute-start.32 = (bf16[3,768,384]{2,1,0:T(8,128)(2,1)}, bf16[3,768,384]{2,1,0:T(8,128)(2,1)}, u32[]{:S(2)}, u32[]{:S(2)}) collective-permute-start(bf16[3,768,384]{2,1,0:T(8,128)(2,1)} %weight_grads.9), channel_id=1, source_target_pairs={{0,8},{1,9},{2,10},{3,11},{4,12},{5,13},{6,14},{7,15},{8,0},{9,1},... | collective-permute-start | bytes 5308424 | tf_op jit(solution)/shard_map/ppermute | solution.py:217
  240.9 65.5 %collective-permute-start.39 = (bf16[5,768,384]{2,1,0:T(8,128)(2,1)}, bf16[5,768,384]{2,1,0:T(8,128)(2,1)}, u32[]{:S(2)}, u32[]{:S(2)}) collective-permute-start(bf16[5,768,384]{2,1,0:T(8,128)(2,1)} %weight_grads.11), channel_id=1, source_target_pairs={{0,8},{1,9},{2,10},{3,11},{4,12},{5,13},{6,14},{7,15},{8,0},{9,1},... | collective-permute-start | bytes 8847368 | tf_op jit(solution)/shard_map/ppermute | solution.py:217
  246.3 13.3 %collective-permute-start.27 = (f32[8,336]{1,0:T(8,128)S(1)}, f32[8,336]{1,0:T(8,128)S(1)}, u32[]{:S(2)}, u32[]{:S(2)}) collective-permute-start(f32[8,336]{1,0:T(8,128)S(1)} %pad_maximum_fusion.16), channel_id=1, source_target_pairs={{0,8},{1,9},{2,10},{3,11},{4,12},{5,13},{6,14},{7,15},{8,0},{9,1},... | collective-permute-start | bytes 32264 | tf_op jit(solution)/shard_map/ppermute | solution.py:217
  246.5 78.5 %collective-permute-start.46 = (bf16[2,768,1024]{2,1,0:T(8,128)(2,1)}, bf16[2,768,1024]{2,1,0:T(8,128)(2,1)}, u32[]{:S(2)}, u32[]{:S(2)}) collective-permute-start(bf16[2,768,1024]{2,1,0:T(8,128)(2,1)} %weight_grads.13), channel_id=1, source_target_pairs={{0,8},{1,9},{2,10},{3,11},{4,12},{5,13},{6,14},{7,15},{8,0},{9,1},... | collective-permute-start | bytes 9437192 | tf_op jit(solution)/shard_map/ppermute | solution.py:217
  256.4 32.5 %collective-permute-start.54 = (bf16[8,1,128,384]{3,2,1,0:T(8,128)(2,1)}, bf16[8,1,128,384]{3,2,1,0:T(8,128)(2,1)}, u32[]{:S(2)}, u32[]{:S(2)}) collective-permute-start(bf16[8,1,128,384]{3,2,1,0:T(8,128)(2,1)} %get-tuple-element.79), channel_id=1, source_target_pairs={{0,16},{1,17},{2,18},{3,19},{4,20},{5,21},{6,22},{7,23},{8,9},{9,8... | collective-permute-start | bytes 2359304 | tf_op jit(solution)/shard_map/ppermute | solution.py:217
  277.5 19.8 %collective-permute-start.31 = (f32[8,336]{1,0:T(8,128)S(1)}, f32[8,336]{1,0:T(8,128)S(1)}, u32[]{:S(2)}, u32[]{:S(2)}) collective-permute-start(f32[8,336]{1,0:T(8,128)S(1)} %add.269), channel_id=1, source_target_pairs={{0,4},{1,5},{2,6},{3,7},{4,0},{5,1},{6,2},{7,3},{8,12},{9,13},{10,... | collective-permute-start | bytes 32264 | tf_op jit(solution)/shard_map/ppermute | solution.py:217
  287.2 15.6 %collective-permute-start.33 = (bf16[8,3,48,384]{3,2,1,0:T(8,128)(2,1)}, bf16[8,3,48,384]{3,2,1,0:T(8,128)(2,1)S(1)}, u32[]{:S(2)}, u32[]{:S(2)}) collective-permute-start(bf16[8,3,48,384]{3,2,1,0:T(8,128)(2,1)} %get-tuple-element.73), channel_id=1, source_target_pairs={{0,16},{1,17},{2,18},{3,19},{4,20},{5,21},{6,22},{7,23},{8,9},{9,8... | collective-permute-start | bytes 2654216 | tf_op jit(solution)/shard_map/ppermute | solution.py:217
  298.4 17.1 %collective-permute-start.56 = (bf16[2,1,128,384]{3,2,1,0:T(8,128)(2,1)S(1)}, bf16[2,1,128,384]{3,2,1,0:T(8,128)(2,1)S(1)}, u32[]{:S(2)}, u32[]{:S(2)}) collective-permute-start(bf16[2,1,128,384]{3,2,1,0:T(8,128)(2,1)S(1)} %get-tuple-element.131), channel_id=1, source_target_pairs={{0,2},{1,3},{2,0},{3,1},{4,6},{5,7},{6,4},{7,5},{8,10},{9,11},{10,... | collective-permute-start | bytes 589832 | tf_op jit(solution)/shard_map/ppermute | solution.py:217
  302.9 19.6 %collective-permute-start.34 = (bf16[4,3,48,384]{3,2,1,0:T(8,128)(2,1)S(1)}, bf16[4,3,48,384]{3,2,1,0:T(8,128)(2,1)S(1)}, u32[]{:S(2)}, u32[]{:S(2)}) collective-permute-start(bf16[4,3,48,384]{3,2,1,0:T(8,128)(2,1)S(1)} %get-tuple-element.109), channel_id=1, source_target_pairs={{0,1},{1,0},{2,3},{3,2},{4,5},{5,4},{6,7},{7,6},{8,24},{9,25},{10,... | collective-permute-start | bytes 1327112 | tf_op jit(solution)/shard_map/ppermute | solution.py:217
  313.9 22.8 %collective-permute-start.40 = (bf16[8,5,48,384]{3,2,1,0:T(8,128)(2,1)}, bf16[8,5,48,384]{3,2,1,0:T(8,128)(2,1)S(1)}, u32[]{:S(2)}, u32[]{:S(2)}) collective-permute-start(bf16[8,5,48,384]{3,2,1,0:T(8,128)(2,1)} %get-tuple-element.75), channel_id=1, source_target_pairs={{0,16},{1,17},{2,18},{3,19},{4,20},{5,21},{6,22},{7,23},{8,9},{9,8... | collective-permute-start | bytes 4423688 | tf_op jit(solution)/shard_map/ppermute | solution.py:217
  332.9 32.5 %collective-permute-start.47 = (bf16[8,2,48,1024]{3,2,1,0:T(8,128)(2,1)}, bf16[8,2,48,1024]{3,2,1,0:T(8,128)(2,1)S(1)}, u32[]{:S(2)}, u32[]{:S(2)}) collective-permute-start(bf16[8,2,48,1024]{3,2,1,0:T(8,128)(2,1)} %get-tuple-element.77), channel_id=1, source_target_pairs={{0,16},{1,17},{2,18},{3,19},{4,20},{5,21},{6,22},{7,23},{8,9},{9,8... | collective-permute-start | bytes 4718600 | tf_op jit(solution)/shard_map/ppermute | solution.py:217
  337.0 28.1 %collective-permute-start.41 = (bf16[4,5,48,384]{3,2,1,0:T(8,128)(2,1)S(1)}, bf16[4,5,48,384]{3,2,1,0:T(8,128)(2,1)S(1)}, u32[]{:S(2)}, u32[]{:S(2)}) collective-permute-start(bf16[4,5,48,384]{3,2,1,0:T(8,128)(2,1)S(1)} %get-tuple-element.107), channel_id=1, source_target_pairs={{0,1},{1,0},{2,3},{3,2},{4,5},{5,4},{6,7},{7,6},{8,24},{9,25},{10,... | collective-permute-start | bytes 2211848 | tf_op jit(solution)/shard_map/ppermute | solution.py:217
  345.5 19.6 %collective-permute-start.37 = (bf16[3,48,384]{2,1,0:T(8,128)(2,1)S(1)}, bf16[3,48,384]{2,1,0:T(8,128)(2,1)S(1)}, u32[]{:S(2)}, u32[]{:S(2)}) collective-permute-start(bf16[3,48,384]{2,1,0:T(8,128)(2,1)S(1)} %fusion.31), channel_id=1, source_target_pairs={{0,16},{1,17},{2,18},{3,19},{4,20},{5,21},{6,22},{7,23},{8,24},{9,... | collective-permute-start | bytes 331784 | tf_op jit(solution)/shard_map/ppermute | solution.py:217
  366.1 19.2 %collective-permute-start.48 = (bf16[4,2,48,1024]{3,2,1,0:T(8,128)(2,1)S(1)}, bf16[4,2,48,1024]{3,2,1,0:T(8,128)(2,1)S(1)}, u32[]{:S(2)}, u32[]{:S(2)}) collective-permute-start(bf16[4,2,48,1024]{3,2,1,0:T(8,128)(2,1)S(1)} %get-tuple-element.105), channel_id=1, source_target_pairs={{0,1},{1,0},{2,3},{3,2},{4,5},{5,4},{6,7},{7,6},{8,24},{9,25},{10,... | collective-permute-start | bytes 2359304 | tf_op jit(solution)/shard_map/ppermute | solution.py:217
  389.0 14.5 %collective-permute-start.45 = (bf16[5,96,384]{2,1,0:T(8,128)(2,1)S(1)}, bf16[5,96,384]{2,1,0:T(8,128)(2,1)S(1)}, u32[]{:S(2)}, u32[]{:S(2)}) collective-permute-start(bf16[5,96,384]{2,1,0:T(8,128)(2,1)S(1)} %pad_maximum_fusion.11), channel_id=1, source_target_pairs={{0,8},{1,9},{2,10},{3,11},{4,12},{5,13},{6,14},{7,15},{8,0},{9,1},... | collective-permute-start | bytes 1105928 | tf_op jit(solution)/shard_map/ppermute | solution.py:217
  (109 other events, 683.7 us)
